TPU v7x, 32 devices: a whole 2x2x4 slice. The times are simulated.
32 devices in a mesh: wide: 8 (over y, x, core), narrow: 4 (over z).
Axes of the slice: x: 2, y: 2, z: 4, core: 2. Of those that a mesh axis runs over, the one named last changes fastest.
Arguments:
- tokens: bfloat16 [8192, 1152], P(('wide', 'narrow')), may hold values from -6 to 6
- condition: bfloat16 [32, 1152], P('wide'), may hold values from -6 to 6
- segment: int32 [8192], P('wide'), may hold values from 0 to 4, as said below
- w_ada: bfloat16 [1152, 6912], P(None, 'narrow'), may hold values from -0.1875 to 0.1875
- b_ada: bfloat16 [6912], P('narrow'), may hold values from -3 to 3
- w_qkv: bfloat16 [1152, 3, 1152], P(None, None, 'narrow'), may hold values from -0.1875 to 0.1875
- w_proj: bfloat16 [1152, 1152], P(None, 'narrow'), may hold values from -0.75 to 0.75
- w_up: bfloat16 [1152, 4608], P(None, 'narrow'), may hold values from -0.1875 to 0.1875
- w_down: bfloat16 [4608, 1152], P('narrow'), may hold values from -0.09375 to 0.09375
- out_grad: bfloat16 [8192, 1152], P(('wide', 'narrow')), may hold values from -6 to 6
Outputs:
- mixed: bfloat16 [8192, 1152], P(('wide', 'narrow'))
- tokens_grad: bfloat16 [8192, 1152], P(('wide', 'narrow'))
- w_ada_grad: float32 [1152, 6912], P('wide', 'narrow')
- b_ada_grad: float32 [6912], P(('narrow', 'wide'))
- w_qkv_grad: float32 [1152, 3, 1152], P('wide', None, 'narrow')
- w_proj_grad: float32 [1152, 1152], P('wide', 'narrow')
- w_up_grad: float32 [1152, 4608], P('wide', 'narrow')
- w_down_grad: float32 [4608, 1152], P(('narrow', 'wide'))
Inputs may be any that keep to these rules, and one draw needn't show every extreme that they name: `segment`: within each wide shard's 1024 rows its 4 image slots lie in order from row 0, each on consecutive rows, with 256 rows (unmasked) or 128 rows (kept tokens of a masked image); the value 4 marks the padding rows after the last image. In every draw some shard has only unmasked images and some shard has padding.
All inputs are finite; a program needn't handle non-finite values.
Results may differ from a plain program's by a relative error of at most 0.02.
Values may be sent and summed in bfloat16 or wider, within the bound.
A program may use at most 128 MiB of HBM per device.

v0:
```python
import jax
import jax.numpy as jnp
from jax import lax
from jax.sharding import PartitionSpec as P

D = 1152
HEADS = 16


norm_epsilon = 1e-06
masked_score = -1e30


def normalize(inputs):
    centred = inputs - jnp.mean(inputs, axis=-1, keepdims=True)
    return centred * lax.rsqrt(jnp.mean(centred * centred, axis=-1, keepdims=True) + norm_epsilon)


def modulate(inputs, scale_rows, shift_rows):
    return normalize(inputs) * (1.0 + scale_rows) + shift_rows


def gelu_tanh(values):
    return jax.nn.gelu(values, approximate=True)


def masked_scores(query_block, seg_block, key_rows, seg_all, factor):
    scores = (
        jnp.einsum("qhe,khe->hqk", query_block, key_rows, preferred_element_type=jnp.float32)
        * factor
    )
    allowed = (seg_block[:, None] == seg_all[None, :])[None, :, :]
    return jnp.where(allowed, scores, masked_score)


def attend_forward(queries, key_rows, value_rows, seg_all, factor):
    row_total, head_count, head_size = queries.shape
    block_rows = min(512, row_total)
    blocks = row_total // block_rows

    def one_block(block_pair):
        query_block, seg_block = block_pair
        scores = masked_scores(query_block, seg_block, key_rows, seg_all, factor)
        row_max = jnp.max(scores, axis=-1, keepdims=True)
        weights = jnp.exp(scores - row_max)
        denominator = jnp.sum(weights, axis=-1, keepdims=True)
        probability = (weights / denominator).astype(jnp.bfloat16)
        result = jnp.einsum(
            "hqk,khe->qhe", probability, value_rows, preferred_element_type=jnp.float32
        )
        return (result, row_max + jnp.log(denominator))

    results, log_sums = lax.map(
        one_block,
        (
            queries.reshape(blocks, block_rows, head_count, head_size),
            seg_all.reshape(blocks, block_rows),
        ),
    )
    return (results.reshape(row_total, head_count, head_size), log_sums)


def attend_backward(queries, key_rows, value_rows, seg_all, log_sums, heads_grad, factor):
    row_total, head_count, head_size = queries.shape
    block_rows = min(512, row_total)
    blocks = row_total // block_rows

    def one_block(running, block_inputs):
        key_grad, value_grad = running
        query_block, seg_block, log_block, grad_block = block_inputs
        scores = masked_scores(query_block, seg_block, key_rows, seg_all, factor)
        probability = jnp.exp(scores - log_block)
        prob_grad = jnp.einsum(
            "qhe,khe->hqk", grad_block, value_rows, preferred_element_type=jnp.float32
        )
        row_inner = jnp.sum(probability * prob_grad, axis=-1, keepdims=True)
        score_grad = (probability * (prob_grad - row_inner)).astype(jnp.bfloat16)
        query_grad = (
            jnp.einsum("hqk,khe->qhe", score_grad, key_rows, preferred_element_type=jnp.float32)
            * factor
        )
        key_grad = (
            key_grad
            + jnp.einsum(
                "hqk,qhe->khe", score_grad, query_block, preferred_element_type=jnp.float32
            )
            * factor
        )
        value_grad = value_grad + jnp.einsum(
            "hqk,qhe->khe",
            probability.astype(jnp.bfloat16),
            grad_block,
            preferred_element_type=jnp.float32,
        )
        return ((key_grad, value_grad), query_grad)

    empty_grad = jnp.zeros(key_rows.shape, jnp.float32)
    block_inputs = (
        queries.reshape(blocks, block_rows, head_count, head_size),
        seg_all.reshape(blocks, block_rows),
        log_sums,
        heads_grad.reshape(blocks, block_rows, head_count, head_size),
    )
    finals, query_grads = lax.scan(one_block, (empty_grad, empty_grad), block_inputs)
    return (query_grads.reshape(row_total, head_count, head_size), finals[0], finals[1])


def shards(tokens, condition, segment, w_ada, b_ada, w_qkv, w_proj, w_up, w_down, out_grad):
    local_rows = tokens.shape[0]
    images = condition.shape[0]
    head_size = D // HEADS
    factor = head_size ** (-0.5)
    narrow_place = lax.axis_index("narrow")
    seg_local = lax.dynamic_slice_in_dim(segment, narrow_place * local_rows, local_rows)
    onehot = (seg_local[:, None] == jnp.arange(images, dtype=jnp.int32)[None, :]).astype(
        jnp.float32
    )
    silu_low = jax.nn.silu(condition.astype(jnp.float32)).astype(jnp.bfloat16)
    mod_part = jnp.dot(silu_low, w_ada, preferred_element_type=jnp.float32) + b_ada.astype(
        jnp.float32
    )
    modulation = lax.all_gather(mod_part, "narrow", axis=1, tiled=True)
    per_token = jnp.dot(onehot, modulation, precision=lax.Precision.HIGHEST)
    shift_one, scale_one, gate_one, shift_two, scale_two, gate_two = jnp.split(per_token, 6, axis=1)
    token_values = tokens.astype(jnp.float32)
    hidden_one, pull_one = jax.vjp(modulate, token_values, scale_one, shift_one)
    hidden_all = lax.all_gather(hidden_one.astype(jnp.bfloat16), "narrow", axis=0, tiled=True)
    projected = jnp.einsum(
        "gd,dcf->gcf", hidden_all, w_qkv, preferred_element_type=jnp.float32
    ).astype(jnp.bfloat16)
    row_total = hidden_all.shape[0]
    head_count = w_qkv.shape[2] // head_size
    queries = projected[:, 0].reshape(row_total, head_count, head_size)
    key_rows = projected[:, 1].reshape(row_total, head_count, head_size)
    value_rows = projected[:, 2].reshape(row_total, head_count, head_size)
    attended, log_sums = attend_forward(queries, key_rows, value_rows, segment, factor)
    heads_low = attended.reshape(row_total, head_count * head_size).astype(jnp.bfloat16)
    chosen = heads_low
    attn_branch = lax.psum_scatter(
        jnp.einsum("gi,oi->go", chosen, w_proj, preferred_element_type=jnp.float32).astype(
            jnp.bfloat16
        ),
        "narrow",
        scatter_dimension=0,
        tiled=True,
    ).astype(jnp.float32)
    middle = token_values + gate_one * attn_branch
    hidden_two, pull_two = jax.vjp(modulate, middle, scale_two, shift_two)
    second_all = lax.all_gather(hidden_two.astype(jnp.bfloat16), "narrow", axis=0, tiled=True)
    up_values = jnp.dot(second_all, w_up, preferred_element_type=jnp.float32)
    activated, gelu_pull = jax.vjp(gelu_tanh, up_values)
    act_low = activated.astype(jnp.bfloat16)
    chosen = act_low
    mlp_branch = lax.psum_scatter(
        jnp.dot(chosen, w_down, preferred_element_type=jnp.float32).astype(jnp.bfloat16),
        "narrow",
        scatter_dimension=0,
        tiled=True,
    ).astype(jnp.float32)
    mixed = (middle + gate_two * mlp_branch).astype(jnp.bfloat16)
    grad_values = out_grad.astype(jnp.float32)
    mlp_grad_low = (gate_two * grad_values).astype(jnp.bfloat16)
    gate_two_grad = grad_values * mlp_branch
    mlp_grad_all = lax.all_gather(mlp_grad_low, "narrow", axis=0, tiled=True)
    w_down_grad = jnp.einsum("gf,gd->fd", act_low, mlp_grad_all, preferred_element_type=jnp.float32)
    act_grad = jnp.einsum("gd,fd->gf", mlp_grad_all, w_down, preferred_element_type=jnp.float32)
    up_grad = gelu_pull(act_grad)[0].astype(jnp.bfloat16)
    w_up_grad = jnp.einsum("gd,gf->df", second_all, up_grad, preferred_element_type=jnp.float32)
    chosen = up_grad
    second_grad = lax.psum_scatter(
        jnp.einsum("gf,df->gd", chosen, w_up, preferred_element_type=jnp.float32).astype(
            jnp.bfloat16
        ),
        "narrow",
        scatter_dimension=0,
        tiled=True,
    ).astype(jnp.float32)
    middle_ln_grad, scale_two_grad, shift_two_grad = pull_two(second_grad)
    middle_grad = grad_values + middle_ln_grad
    attn_grad_low = (gate_one * middle_grad).astype(jnp.bfloat16)
    gate_one_grad = middle_grad * attn_branch
    attn_grad_all = lax.all_gather(attn_grad_low, "narrow", axis=0, tiled=True)
    w_proj_grad = jnp.einsum(
        "go,gi->oi", attn_grad_all, heads_low, preferred_element_type=jnp.float32
    )
    heads_grad = jnp.einsum(
        "go,oi->gi", attn_grad_all, w_proj, preferred_element_type=jnp.float32
    ).astype(jnp.bfloat16)
    query_grad, key_grad, value_grad = attend_backward(
        queries,
        key_rows,
        value_rows,
        segment,
        log_sums,
        heads_grad.reshape(row_total, head_count, head_size),
        factor,
    )
    qkv_grad = (
        jnp.stack([query_grad, key_grad, value_grad], axis=1)
        .reshape(row_total, 3, head_count * head_size)
        .astype(jnp.bfloat16)
    )
    w_qkv_grad = jnp.einsum("gd,gcf->dcf", hidden_all, qkv_grad, preferred_element_type=jnp.float32)
    chosen = qkv_grad
    first_grad = lax.psum_scatter(
        jnp.einsum("gcf,dcf->gd", chosen, w_qkv, preferred_element_type=jnp.float32).astype(
            jnp.bfloat16
        ),
        "narrow",
        scatter_dimension=0,
        tiled=True,
    ).astype(jnp.float32)
    token_ln_grad, scale_one_grad, shift_one_grad = pull_one(first_grad)
    tokens_grad = (middle_grad + token_ln_grad).astype(jnp.bfloat16)
    per_token_grad = jnp.concatenate(
        [
            shift_one_grad,
            scale_one_grad,
            gate_one_grad,
            shift_two_grad,
            scale_two_grad,
            gate_two_grad,
        ],
        axis=1,
    )
    mod_grad_part = jnp.einsum("ri,rc->ic", onehot, per_token_grad, precision=lax.Precision.HIGHEST)
    mod_grad = lax.psum_scatter(
        mod_grad_part.astype(jnp.bfloat16), "narrow", scatter_dimension=1, tiled=True
    )
    w_ada_grad = jnp.einsum("id,ic->dc", silu_low, mod_grad, preferred_element_type=jnp.float32)
    b_ada_grad = jnp.sum(mod_grad.astype(jnp.float32), axis=0)
    w_ada_grad, b_ada_grad, w_qkv_grad, w_proj_grad, w_up_grad, w_down_grad = (
        lax.psum_scatter(w_ada_grad, "wide", scatter_dimension=0, tiled=True),
        lax.psum_scatter(b_ada_grad, "wide", scatter_dimension=0, tiled=True),
        lax.psum_scatter(w_qkv_grad, "wide", scatter_dimension=0, tiled=True),
        lax.psum_scatter(w_proj_grad, "wide", scatter_dimension=0, tiled=True),
        lax.psum_scatter(w_up_grad, "wide", scatter_dimension=0, tiled=True),
        lax.psum_scatter(w_down_grad, "wide", scatter_dimension=0, tiled=True),
    )
    return (
        mixed,
        tokens_grad,
        w_ada_grad,
        b_ada_grad,
        w_qkv_grad,
        w_proj_grad,
        w_up_grad,
        w_down_grad,
    )


def solution(mesh):
    placed = (
        P(("wide", "narrow"), None),
        P("wide", None),
        P("wide"),
        P(None, "narrow"),
        P("narrow"),
        P(None, None, "narrow"),
        P(None, "narrow"),
        P(None, "narrow"),
        P("narrow", None),
        P(("wide", "narrow"), None),
    )
    return jax.shard_map(
        shards,
        mesh=mesh,
        in_specs=placed,
        out_specs=(
            P(("wide", "narrow"), None),
            P(("wide", "narrow"), None),
            P("wide", "narrow"),
            P(("narrow", "wide")),
            P("wide", None, "narrow"),
            P("wide", "narrow"),
            P("wide", "narrow"),
            P(("narrow", "wide"), None),
        ),
        check_vma=False,
    )
```

profile of v0, /device:TPU:0, one launch (start us, length us, event | category | flops | bytes accessed | tf_op | source)
XLA Modules:
  0.0 895.3 jit_solution(6575222553533540719)
XLA Ops:
  14.0 15.1 %all-gather = f32[4,1728,4]{1,2,0:T(4,128)S(1)} all-gather(f32[1,1728,4]{1,2,0:T(4,128)S(1)} %fusion.52), channel_id=1, replica_groups=mesh['wide'=8,'narrow'=4] {'narrow'}, dimensions={0}, use_global_device_ids=true | all-gather | bytes 138240 | tf_op jit(solution)/shard_map/all_gather | solution.py:122
  37.2 51.5 %all-gather.6.cloned.1.call-done = bf16[1024,1152]{1,0:T(8,128)(2,1)} async-done(((bf16[256,1152]{1,0:T(8,128)(2,1)}), bf16[1024,1152]{1,0:T(8,128)(2,1)}) %all-gather.6.cloned.1.call-update) | async-done | bytes 2359312 | tf_op jit(solution)/shard_map/all_gather | solution.py:127
  100.3 19.1 %while.27 = (s32[]{:T(128)}, bf16[2,512,4,72]{1,3,2,0:T(8,128)(2,1)}, f32[2,4,512,1]{2,1,3,0:T(4,128)S(1)}, s32[2,512]{1,0:T(2,128)S(1)}, s32[1024]{0:T(1024)S(1...) while((s32[]{:T(128)}, ...), condition=%wide.region_5.6_spmd, body=%wide.region_2.5_spmd.sunk | while | flops 629667840 | bytes 36481224 | solution.py:53
  125.2 47.0 %reduce-scatter.13.cloned.1.call-done = bf16[256,1152]{1,0:T(8,128)(2,1)} async-done(((bf16[1024,1152]{1,0:T(8,128)(2,1)}), bf16[256,1152]{1,0:T(8,128)(2,1)}) %reduce-scatter.13.cloned.1.call-update) | async-done | bytes 589840 | tf_op jit(solution)/shard_map/reduce_scatter | solution.py:139
  178.9 49.1 %all-gather.10.cloned.1.call-done = bf16[1024,1152]{1,0:T(8,128)(2,1)} async-done(((bf16[256,1152]{1,0:T(8,128)(2,1)}), bf16[1024,1152]{1,0:T(8,128)(2,1)}) %all-gather.10.cloned.1.call-update) | async-done | bytes 2359312 | tf_op jit(solution)/shard_map/all_gather | solution.py:164
  227.9 8.1 fusion.92
  236.1 43.2 %all-gather.8.cloned.1.call-done = bf16[1024,1152]{1,0:T(8,128)(2,1)} async-done(((bf16[256,1152]{1,0:T(8,128)(2,1)}), bf16[1024,1152]{1,0:T(8,128)(2,1)}) %all-gather.8.cloned.1.call-update) | async-done | bytes 2359312 | tf_op jit(solution)/shard_map/all_gather | solution.py:149
  279.3 10.3 %fusion.47 = (bf16[1024,1152]{1,0:T(8,128)(2,1)S(1)}, f32[1024,1152]{1,0:T(8,128)}) fusion(f32[1024,1152]{1,0:T(8,128)} %fusion.92, bf16[1024,1152]{1,0:T(8,128)(2,1)} %all-gather.8.cloned.1.call-done, bf16[1152,1152]{1,0:T(8,128)(2,1)S(1)} %copy-done), kind=kOutput, calls=%fused_computation.59 | convolution fusion | flops 2741501952 | bytes 16809984 | tf_op jit(solution)/shard_map/dot_general | solution.py:150
  295.9 8.7 convolution_convert_fusion.3
  304.7 38.1 %reduce-scatter.17.cloned.1.call-done = bf16[256,1152]{1,0:T(8,128)(2,1)} async-done(((bf16[1024,1152]{1,0:T(8,128)(2,1)}), bf16[256,1152]{1,0:T(8,128)(2,1)}) %reduce-scatter.17.cloned.1.call-update) | async-done | bytes 589840 | tf_op jit(solution)/shard_map/reduce_scatter | solution.py:170
  344.6 48.0 %reduce-scatter.15.cloned.1.call-done = bf16[256,1152]{1,0:T(8,128)(2,1)} async-done(((bf16[1024,1152]{1,0:T(8,128)(2,1)}), bf16[256,1152]{1,0:T(8,128)(2,1)}) %reduce-scatter.15.cloned.1.call-update) | async-done | bytes 589840 | tf_op jit(solution)/shard_map/reduce_scatter | solution.py:154
  399.0 49.9 %all-gather.12.cloned.1.call-done = bf16[1024,1152]{1,0:T(8,128)(2,1)} async-done(((bf16[256,1152]{1,0:T(8,128)(2,1)}), bf16[1024,1152]{1,0:T(8,128)(2,1)}) %all-gather.12.cloned.1.call-update) | async-done | bytes 2359312 | tf_op jit(solution)/shard_map/all_gather | solution.py:182
  456.4 25.7 %while.28 = (s32[]{:T(128)}, f32[1024,4,72]{0,2,1:T(8,128)S(1)}, f32[1024,4,72]{0,2,1:T(8,128)}, bf16[2,512,4,72]{1,3,2,0:T(8,128)(2,1)}, bf16[2,512,4,72]{1,3,2...) while((s32[]{:T(128)}, f32[1024,4,72]{0,2,1:T(8,128)S(1)}, ...), condition=%wide.region_15.16_spmd.clone, body=%wide.region_13.15_spmd.clone.sunk | while | flops 1543550976 | bytes 92211544 | solution.py:104
  491.6 46.9 %reduce-scatter.19.cloned.1.call-done = bf16[256,1152]{1,0:T(8,128)(2,1)} async-done(((bf16[1024,1152]{1,0:T(8,128)(2,1)}), bf16[256,1152]{1,0:T(8,128)(2,1)}) %reduce-scatter.19.cloned.1.call-update) | async-done | bytes 589840 | tf_op jit(solution)/shard_map/reduce_scatter | solution.py:205
  550.0 7.4 fusion.94
  559.0 8.3 fusion.87
  572.8 7.3 fusion.48
  580.1 7.3 reduce-scatter.31.cloned.1.call-done
  595.3 13.7 %all-reduce = f32[1728]{0:T(1024)S(1)} all-reduce(f32[1728]{0:T(1024)S(1)} %convert_reduce_fusion.1), channel_id=8, replica_groups=mesh['wide'=8,'narrow'=4] {'wide'}, use_global_device_ids=true, to_apply=%region_22.23.clone | all-reduce | flops 1728 | bytes 13824
  609.6 38.1 %reduce-scatter.27.cloned.1.call-done = f32[144,1152]{1,0:T(8,128)} async-done(((f32[1152,1152]{1,0:T(8,128)}), f32[144,1152]{1,0:T(8,128)}) %reduce-scatter.27.cloned.1.call-update) | async-done | bytes 663568 | tf_op jit(solution)/shard_map/reduce_scatter | solution.py:237
  647.7 60.9 %reduce-scatter.29.cloned.1.call-done = f32[144,1152]{1,0:T(8,128)} async-done(((f32[1152,1152]{1,0:T(8,128)}), f32[144,1152]{1,0:T(8,128)}) %reduce-scatter.29.cloned.1.call-update) | async-done | bytes 663568 | tf_op jit(solution)/shard_map/reduce_scatter | solution.py:238
  708.7 43.6 %reduce-scatter.25.cloned.1.call-done = f32[144,288]{1,0:T(8,128)} async-done(((f32[1152,288]{1,0:T(8,128)}), f32[144,288]{1,0:T(8,128)}) %reduce-scatter.25.cloned.1.call-update) | async-done | bytes 165904 | tf_op jit(solution)/shard_map/reduce_scatter | solution.py:236
  752.3 61.3 %reduce-scatter.23.cloned.1.call-done = f32[144,3,288]{2,0,1:T(8,128)} async-done(((f32[1152,3,288]{2,0,1:T(8,128)}), f32[144,3,288]{2,0,1:T(8,128)}) %reduce-scatter.23.cloned.1.call-update) | async-done | bytes 497680 | tf_op jit(solution)/shard_map/reduce_scatter | solution.py:235
  813.6 74.7 %reduce-scatter.21.cloned.1.call-done = f32[144,1728]{1,0:T(8,128)} async-done(((f32[1152,1728]{1,0:T(8,128)}), f32[144,1728]{1,0:T(8,128)}) %reduce-scatter.21.cloned.1.call-update) | async-done | bytes 995344 | tf_op jit(solution)/shard_map/reduce_scatter | solution.py:233
  (241 shorter events, 140.5 us)
Async XLA Ops:
  7.2 272.1 %copy-start = (bf16[1152,1152]{1,0:T(8,128)(2,1)S(1)}, bf16[1152,1152]{1,0:T(8,128)(2,1)}, u32[]{:S(2)}) copy-start(bf16[1152,1152]{1,0:T(8,128)(2,1)} %param.21) | copy-start | bytes 7962628
  7.2 81.6 %all-gather.6.cloned.1.call-start = ((), (), s32[]{:S(2)}) async-start(), calls=%async_computation.10 | async-start | bytes 2949120 | tf_op jit(solution)/shard_map/all_gather | solution.py:127
  8.6 24.2 %copy-start.41 = (f32[256]{0:T(256)}, f32[256]{0:T(256)S(1)}, u32[]{:S(2)}) copy-start(f32[256]{0:T(256)S(1)} %broadcast_multiply_fusion.1) | copy-start | bytes 3076
  10.0 22.8 %copy-start.45 = (f32[256]{0:T(256)}, f32[256]{0:T(256)S(1)}, u32[]{:S(2)}) copy-start(f32[256]{0:T(256)S(1)} %fusion.79) | copy-start | bytes 3076
  36.9 135.2 %reduce-scatter.13.cloned.1.call-start = ((), (), s32[]{:S(2)}) async-start(), calls=%async_computation.11 | async-start | bytes 2949120 | tf_op jit(solution)/shard_map/reduce_scatter | solution.py:139
  125.1 102.8 %all-gather.10.cloned.1.call-start = ((), (), s32[]{:S(2)}) async-start(), calls=%async_computation.14 | async-start | bytes 2949120 | tf_op jit(solution)/shard_map/all_gather | solution.py:164
  177.8 101.4 %all-gather.8.cloned.1.call-start = ((), (), s32[]{:S(2)}) async-start(), calls=%async_computation.12 | async-start | bytes 2949120 | tf_op jit(solution)/shard_map/all_gather | solution.py:149
  178.4 164.4 %reduce-scatter.17.cloned.1.call-start = ((), (), s32[]{:S(2)}) async-start(), calls=%async_computation.15 | async-start | bytes 2949120 | tf_op jit(solution)/shard_map/reduce_scatter | solution.py:170
  295.8 96.7 %reduce-scatter.15.cloned.1.call-start = ((), (), s32[]{:S(2)}) async-start(), calls=%async_computation.13 | async-start | bytes 2949120 | tf_op jit(solution)/shard_map/reduce_scatter | solution.py:154
  304.6 38.2 %copy-start.5 = (f32[256,1152]{1,0:T(8,128)S(1)}, f32[256,1152]{1,0:T(8,128)}, u32[]{:S(2)}) copy-start(f32[256,1152]{1,0:T(8,128)} %copy-done.4) | copy-start | bytes 3538948
  304.6 144.2 %all-gather.12.cloned.1.call-start = ((), (), s32[]{:S(2)}) async-start(), calls=%async_computation.16 | async-start | bytes 2949120 | tf_op jit(solution)/shard_map/all_gather | solution.py:182
  395.9 52.9 %copy-start.11 = (f32[256,1152]{1,0:T(8,128)}, f32[256,1152]{1,0:T(8,128)S(1)}, u32[]{:S(2)}) copy-start(f32[256,1152]{1,0:T(8,128)S(1)} %get-tuple-element.249) | copy-start | bytes 3538948
  398.7 139.8 %reduce-scatter.19.cloned.1.call-start = ((), (), s32[]{:S(2)}) async-start(), calls=%async_computation.17 | async-start | bytes 2949120 | tf_op jit(solution)/shard_map/reduce_scatter | solution.py:205
  491.5 47.0 %copy-start.10 = (bf16[256,1152]{1,0:T(8,128)(2,1)S(1)}, bf16[256,1152]{1,0:T(8,128)(2,1)}, u32[]{:S(2)}) copy-start(bf16[256,1152]{1,0:T(8,128)(2,1)} %param.14) | copy-start | bytes 1769476
  491.5 47.0 %copy-start.42 = (f32[256]{0:T(256)S(1)}, f32[256]{0:T(256)}, u32[]{:S(2)}) copy-start(f32[256]{0:T(256)} %copy-done.41) | copy-start | bytes 3076
  491.5 48.9 %copy-start.44 = (f32[256]{0:T(256)S(1)}, f32[256]{0:T(256)}, u32[]{:S(2)}) copy-start(f32[256]{0:T(256)} %copy-done.43) | copy-start | bytes 3076
  491.5 48.9 %copy-start.46 = (f32[256]{0:T(256)S(1)}, f32[256]{0:T(256)}, u32[]{:S(2)}) copy-start(f32[256]{0:T(256)} %copy-done.45) | copy-start | bytes 3076
  491.5 95.9 %reduce-scatter.31.cloned.1.call-start = ((), (), s32[]{:S(2)}) async-start(), calls=%async_computation.23 | async-start | bytes 2211840
  549.4 98.3 %reduce-scatter.27.cloned.1.call-start = ((), (), s32[]{:S(2)}) async-start(), calls=%async_computation.21 | async-start | bytes 5971968 | tf_op jit(solution)/shard_map/reduce_scatter | solution.py:237
  557.4 151.3 %reduce-scatter.29.cloned.1.call-start = ((), (), s32[]{:S(2)}) async-start(), calls=%async_computation.22 | async-start | bytes 5971968 | tf_op jit(solution)/shard_map/reduce_scatter | solution.py:238
  567.4 184.9 %reduce-scatter.25.cloned.1.call-start = ((), (), s32[]{:S(2)}) async-start(), calls=%async_computation.20 | async-start | bytes 1990656 | tf_op jit(solution)/shard_map/reduce_scatter | solution.py:236
  572.7 240.9 %reduce-scatter.23.cloned.1.call-start = ((), (), s32[]{:S(2)}) async-start(), calls=%async_computation.19 | async-start | bytes 5971968 | tf_op jit(solution)/shard_map/reduce_scatter | solution.py:235
  580.1 308.3 %reduce-scatter.21.cloned.1.call-start = ((), (), s32[]{:S(2)}) async-start(), calls=%async_computation.18 | async-start | bytes 9289728 | tf_op jit(solution)/shard_map/reduce_scatter | solution.py:233
  593.0 295.4 %copy-start.1 = (bf16[1152,1152]{1,0:T(8,128)(2,1)S(1)}, bf16[1152,1152]{1,0:T(8,128)(2,1)}, u32[]{:S(2)}) copy-start(bf16[1152,1152]{1,0:T(8,128)(2,1)} %param.21) | copy-start | bytes 7962628
  (52 other events, 159.7 us)
Sparse Core Ops, SparseCore 0:
  37.1 51.6 all-gather.5
  125.2 46.8 reduce-scatter.12
  177.9 49.9 all-gather.9
  229.9 49.2 all-gather.7
  296.0 46.8 reduce-scatter.16
  345.0 47.5 reduce-scatter.14
  398.8 49.9 all-gather.11
  491.6 46.8 reduce-scatter.18
  549.5 37.8 reduce-scatter.30
  591.6 56.0 reduce-scatter.26
  651.7 56.9 reduce-scatter.28
  712.8 39.3 reduce-scatter.24
  756.6 56.9 reduce-scatter.22
  817.7 70.6 reduce-scatter.20
where the time goes:
time: 900 us; the launch traced here: 895 us
  waiting for transfers between devices  660 us (73%)
  matrix products  120 us (13%)
  other arithmetic  35 us (4%)
  local copies, waits for them, and re-layouts  33 us (4%)
  blocking collectives  28.8 us (3%)
  between operations  15.5 us (2%)
    reduce_scatter x1, waiting for transfers between devices, shards(): lax.psum_scatter(w_ada_grad, 'wide', scatter_dimension=0, tiled=True)  74.7 us
    reduce_scatter x1, waiting for transfers between devices, shards(): lax.psum_scatter(w_qkv_grad, 'wide', scatter_dimension=0, tiled=True)  61.3 us
    reduce_scatter x1, waiting for transfers between devices, shards(): lax.psum_scatter(w_down_grad, 'wide', scatter_dimension=0, tiled=True)  60.9 us
    all_gather x1, waiting for transfers between devices, shards(): lax.all_gather(hidden_one.astype(jnp.bfloat16), 'narrow', axis=0, tiled=T...  51.5 us
    all_gather x1, waiting for transfers between devices, shards(): attn_grad_all = lax.all_gather(attn_grad_low, 'narrow', axis=0, tiled=True)  49.9 us
    all_gather x1, waiting for transfers between devices, shards(): mlp_grad_all = lax.all_gather(mlp_grad_low, 'narrow', axis=0, tiled=True)  49.1 us
    reduce_scatter x1, waiting for transfers between devices, shards(): lax.psum_scatter(jnp.dot(chosen, w_down, preferred_element_type=jnp.float...  48 us
    reduce_scatter x1, waiting for transfers between devices, shards(): lax.psum_scatter(jnp.einsum('gi,oi->go', chosen, w_proj, preferred_elemen...  47 us
  transfers between devices with their start and end apart: 14, of which 14 were waited for; matrix products, arithmetic and copies ran while one was open for 6% of the time, Pallas kernels for 0%

commit v1 on v0

v1 whole, which is shorter than its diff:
```python
import functools
import math

import jax
import jax.numpy as jnp
from jax import lax
from jax.experimental import pallas as pl
from jax.experimental.pallas import tpu as pltpu
from jax.sharding import PartitionSpec as P

D = 1152
HEAD = 72
HEADS_LOCAL = 4
QUARTER = 288
HALF = 576
BLK = 144
SUB_A = 80
SEG = 128
OWN = 256
GROUP = 512
ATT = 640
NEG = -1e30
EPS = 1e-6
FACTOR = HEAD ** -0.5
GELU_ONE = math.sqrt(2.0 / math.pi)
GELU_TWO = 0.044715

f32, bf16 = jnp.float32, jnp.bfloat16
MESH = pl.DeviceIdType.MESH
NN = (((1,), (0,)), ((), ()))
NT = (((1,), (1,)), ((), ()))
TN = (((0,), (0,)), ((), ()))
WINDOWS = ((0, 128), (0, 256), (128, 128), (128, 256))


def dot(a, b, dims):
    return lax.dot_general(a, b, dims, preferred_element_type=f32)


def rows_at(start, size, align=16):
    return pl.ds(pl.multiple_of(start, align), size)


def mean_row(v):
    return jnp.sum(v, axis=-1, keepdims=True) * (1.0 / D)


def norm_parts(v):
    centred = v - mean_row(v)
    scale = lax.rsqrt(mean_row(centred * centred) + EPS)
    return centred * scale, scale


def norm_back(normal, scale, e):
    return scale * (e - mean_row(e) - normal * mean_row(e * normal))


def head_mask(hd, rows):
    start, width = WINDOWS[hd]
    low = HEAD * hd - start
    lane = lax.broadcasted_iota(jnp.int32, (rows, width), 1)
    return (lane >= low) & (lane < low + HEAD)


class Names:
    def __init__(self):
        self.ids = {}

    def __call__(self, *name):
        return self.ids.setdefault(name, len(self.ids))


SEMS = 160


def kernel(
    gather_wide, step,
    seg, cond, bada, tok_h, og_h, wada_h, wqkv_h, wproj_h, wup_h, wdown_h,
    mixed_o, tg_o, gw_o, mod_o, wada_o, bada_o,
    wt, crecv, frecv, srecv, zrecv, tok, og, h1, qkv, heads, lse_t, attp, attr, h2, mlpg, big,
    mlpp, mlpr, seco, secr, mgrad, attg, hgrad, facc, firstr, modblk, modrecv, silu_all, msum, mgr, mall, silu8,
    ssem, rsem, lsem,
):
    w = lax.axis_index("wide")
    n = lax.axis_index("narrow")
    b = w // step
    bits = (b % 2, (b // 2) % 2, b // 4)
    low, high = n % 2, n // 2

    def narrow_to(mask):
        m = n
        if mask & 1:
            m = m + 1 - 2 * low
        if mask & 2:
            m = m + 2 - 4 * high
        return (w, m)

    def wide_to(mask):
        m = w
        for k in range(3):
            if mask & (1 << k):
                m = m + step * (1 << k) * (1 - 2 * bits[k])
        return (m, n)

    def block_of(mask):
        m = b
        for k in range(3):
            if mask & (1 << k):
                m = m + (1 << k) * (1 - 2 * bits[k])
        return m

    names = Names()

    def remote(name, src, dst, dev):
        k = names(*name)
        return pltpu.make_async_remote_copy(
            src_ref=src, dst_ref=dst, send_sem=ssem.at[k], recv_sem=rsem.at[k], device_id=dev, device_id_type=MESH
        )

    sends = {}

    def send(name, src, dst, dev):
        copy = remote(name, src, dst, dev)
        copy.start()
        sends[name] = copy

    def recv(name, landing):
        remote(name, landing, landing, narrow_to(1)).wait_recv()

    def sent(prefix):
        for name in [s for s in sends if s[: len(prefix)] == prefix]:
            sends.pop(name).wait_send()

    locals_ = Names()

    def load(name, src, dst):
        copy = pltpu.make_async_copy(src, dst, lsem.at[locals_(name)])
        copy.start()
        return copy

    off = 128 * high
    own_at = off + OWN * low
    other_at = off + OWN * (1 - low)
    halo_at = GROUP * (1 - high)
    halo_there = GROUP * high

    load_a = load("a", wqkv_h, wt.at[0, pl.ds(0, 3 * QUARTER)])
    load_b = load("b", wproj_h, wt.at[0, pl.ds(3 * QUARTER, QUARTER)])
    load_m = load("m", wada_h, big.at[pl.ds(0, 3 * HALF)])
    load_t = load("t", tok_h, tok.at[rows_at(own_at, OWN)])
    load_u = load("u", wup_h, wt.at[1])
    load_d = load("d", wdown_h, wt.at[2])
    load_g = load("g", og_h, og.at[rows_at(OWN * low, OWN)])

    barrier = pltpu.get_barrier_semaphore()
    partners = [narrow_to(m) for m in (1, 2, 3)] + [wide_to(m) for m in (range(1, 8) if gather_wide else (1, 2, 4))]
    for dev in partners:
        pl.semaphore_signal(barrier, inc=1, device_id=dev, device_id_type=MESH)
    pl.semaphore_wait(barrier, len(partners))

    def block_rows(mask, part=None):
        base = block_of(mask) * BLK
        if part is None:
            return rows_at(base, BLK)
        return rows_at(base, SUB_A) if part == 0 else rows_at(base + SUB_A, BLK - SUB_A)

    def ag_z(m):
        r = block_rows(0)
        send(("ag", m, "z"), wt.at[m, r], wt.at[3 + m, r], narrow_to(2))

    def ag_one(m):
        recv(("ag", m, "z"), wt.at[3 + m, block_rows(0)])
        for part, axis in ((0, 2), (1, 4)):
            r = block_rows(0, part)
            send(("ag", m, "1", part), wt.at[3 + m, r], wt.at[3 + m, r], wide_to(axis))

    def ag_two(m):
        for part, axis, other in ((0, 2, 4), (1, 4, 2)):
            recv(("ag", m, "1", part), wt.at[3 + m, block_rows(axis, part)])
            for i, mask in enumerate((0, axis)):
                r = block_rows(mask, part)
                send(("ag", m, "2", part, i), wt.at[3 + m, r], wt.at[3 + m, r], wide_to(other))

    def ag_three(m):
        for part, axis, other in ((0, 2, 4), (1, 4, 2)):
            for i, mask in enumerate((other, 6)):
                recv(("ag", m, "2", part, i), wt.at[3 + m, block_rows(mask, part)])
        for i, mask in enumerate((0, 2, 4, 6)):
            r = block_rows(mask)
            send(("ag", m, "3", i), wt.at[3 + m, r], wt.at[3 + m, r], wide_to(1))

    def ag_end(m):
        for i, mask in enumerate((1, 3, 5, 7)):
            recv(("ag", m, "3", i), wt.at[3 + m, block_rows(mask)])

    load_a.wait()
    load_b.wait()
    ag_z(0)
    send(("tok",), tok_h, tok.at[rows_at(own_at, OWN)], narrow_to(1))
    halo_first = remote(
        ("halo", 0), tok_h.at[rows_at(128 * (1 - high), SEG)], tok.at[rows_at(halo_there, SEG)], narrow_to(2)
    )
    halo_second = remote(
        ("halo", 1), tok.at[rows_at(halo_at, SEG)], tok.at[rows_at(halo_at, SEG)], narrow_to(1)
    )
    halo_source = low != high

    @pl.when(halo_source)
    def _():
        halo_first.start()

    c = cond[...].astype(f32)
    silu = (c / (1.0 + jnp.exp(-c))).astype(bf16).astype(f32)
    silu8[...] = jnp.zeros((16, D), f32)
    silu8[0:4, :] = silu
    if gather_wide:
        silu_all[b] = silu8[0:8, :]
        for mask in range(1, 8):
            send(("silu", mask), silu8.at[pl.ds(0, 8)], silu_all.at[b], wide_to(mask))
    load_m.wait()
    silu_low = silu8[...].astype(bf16)
    row8 = lax.broadcasted_iota(jnp.int32, (8, HALF), 0)
    for i in range(3):
        part = dot(silu_low, big[HALF * i : HALF * (i + 1), :], NT)[0:8, :] + bada[i : i + 1, :]
        modrecv[3 * n + i, :, 0:HALF] = jnp.where(row8 < 4, part, 0.0)
        modrecv[3 * n + i, :, HALF:ATT] = jnp.zeros((8, ATT - HALF), f32)
    for mask in (1, 2, 3):
        mine = modrecv.at[pl.ds(3 * n, 3)]
        send(("mod", mask), mine, mine, narrow_to(mask))
    load_u.wait()
    ag_z(1)
    load_d.wait()
    ag_z(2)
    load_g.wait()
    send(("og",), og_h, og.at[rows_at(OWN * low, OWN)], narrow_to(1))
    for mask in (1, 2, 3):
        m = narrow_to(mask)[1]
        recv(("mod", mask), modrecv.at[pl.ds(3 * m, 3)])
    for k in range(6):
        first = modrecv[2 * k]
        second = pltpu.roll(modrecv[2 * k + 1], 64, 1)
        modblk[k, :, 0:512] = first[:, 0:512]
        modblk[k, :, 512:640] = first[:, 512:640] + second[:, 0:128]
        modblk[k, :, 640:D] = second[:, 128:640]

    def mod_row(k, shard_block):
        return modblk[k, pl.ds(seg[shard_block * SEG], 1), :]

    def first_norm(base, size):
        def body(t, carry):
            r = rows_at(base + t * 32, 32, 32)
            block = 3 * high + (base + t * 32) // SEG
            normal, _ = norm_parts(tok[r, :].astype(f32))
            h1[r, :] = (normal * (1.0 + mod_row(1, block)) + mod_row(0, block)).astype(bf16)
            return carry

        lax.fori_loop(0, size // 32, body, 0)

    load_t.wait()
    first_norm(own_at, OWN)
    ag_one(0)
    recv(("tok",), tok.at[rows_at(other_at, OWN)])
    first_norm(other_at, OWN)

    @pl.when(jnp.logical_not(halo_source))
    def _():
        halo_first.wait_recv()
        halo_second.start()

    @pl.when(halo_source)
    def _():
        halo_second.wait_recv()
        halo_first.wait_send()

    first_norm(halo_at, SEG)

    @pl.when(jnp.logical_not(halo_source))
    def _():
        halo_second.wait_send()

    ag_two(0)

    def project(s):
        def body(i, carry):
            qkv[s, i] = dot(h1[...], wt[3 * s, rows_at(QUARTER * i, 384), :], NT).astype(bf16)
            return carry

        lax.fori_loop(0, 3, body, 0)

    def key_bias(j, k0, count):
        mine = seg[SEG * (j + 3 * high)]
        return [jnp.where(seg[SEG * (k0 + i + 3 * high)] == mine, 0.0, NEG) for i in range(count)]

    def attend(s, j, k0, count):
        r = rows_at(j * SEG, SEG, SEG)
        keys = slice(k0 * SEG, (k0 + count) * SEG)
        bias = key_bias(j, k0, count)
        out = [jnp.zeros((SEG, 128), f32) for _ in range(3)]
        lse = jnp.zeros((SEG, 128), f32)
        lane = lax.broadcasted_iota(jnp.int32, (SEG, 128), 1)
        for hd, (a, width) in enumerate(WINDOWS):
            mask = head_mask(hd, SEG)
            q = jnp.where(mask, qkv[s, 0, r, a : a + width].astype(f32), 0.0).astype(bf16)
            scores = dot(q, qkv[s, 1, keys, a : a + width], NT) * FACTOR
            scores = jnp.concatenate(
                [scores[:, i * SEG : (i + 1) * SEG] + bias[i] for i in range(count)], axis=1
            )
            top = jnp.max(scores, axis=1, keepdims=True)
            weights = jnp.exp(scores - top)
            total = jnp.sum(weights, axis=1, keepdims=True)
            prob = (weights * (1.0 / total)).astype(bf16)
            res = jnp.where(mask, dot(prob, qkv[s, 2, keys, a : a + width], NN), 0.0)
            for i in range(width // 128):
                out[a // 128 + i] += res[:, i * 128 : (i + 1) * 128]
            lse = jnp.where(lane == hd, top + jnp.log(total), lse)
        for i in range(3):
            heads[s, r, i * 128 : (i + 1) * 128] = out[i].astype(bf16)
        lse_t[s, :, r] = lse.T[0:8, :]

    def for_blocks(fn):
        fn(0, 0, 2)
        fn(1, 0, 5)

        def body(j, carry):
            fn(j, 1, 4)
            return carry

        lax.fori_loop(2, 5, body, 0)

    project(0)
    ag_three(0)
    ag_one(1)
    for_blocks(functools.partial(attend, 0))
    ag_end(0)
    ag_two(1)
    project(1)
    ag_one(2)
    ag_three(1)
    for_blocks(functools.partial(attend, 1))
    ag_two(2)

    def order(i):
        return 1 - high if i == 0 else high

    for i in range(2):
        cc = order(i)
        src = rows_at(off + OWN * cc, OWN)
        dst = rows_at(OWN * cc, OWN)

        def body(t, carry):
            cols = pl.ds(pl.multiple_of(t * 384, 128), 384)
            part = dot(heads[0, src, 0:QUARTER], wt[0, 3 * QUARTER : D, cols], NN)
            part += dot(heads[1, src, 0:QUARTER], wt[3, 3 * QUARTER : D, cols], NN)
            attp[dst, cols] = part.astype(bf16)
            return carry

        lax.fori_loop(0, 3, body, 0)
        send(("att", i), attp.at[dst], attr.at[dst], narrow_to(1))

    ag_three(2)
    ag_end(1)
    ag_end(2)
    recv(("og",), og.at[rows_at(OWN * (1 - low), OWN)])

    for i in range(2):
        cc = order(i)
        chunk = rows_at(OWN * cc, OWN)
        recv(("att", i), attr.at[chunk])

        def second_norm(t, carry):
            r = rows_at(OWN * cc + t * 32, 32, 32)
            ra = rows_at(off + OWN * cc + t * 32, 32, 32)
            block = 4 * high + 2 * cc + t // 4
            branch = attp[r, :].astype(f32) + attr[r, :].astype(f32)
            middle = tok[ra, :].astype(f32) + mod_row(2, block) * branch
            normal, _ = norm_parts(middle)
            h2[r, :] = (normal * (1.0 + mod_row(4, block)) + mod_row(3, block)).astype(bf16)
            mlpg[r, :] = (mod_row(5, block) * og[r, :].astype(f32)).astype(bf16)
            return carry

        lax.fori_loop(0, OWN // 32, second_norm, 0)

        def units(k, carry):
            s, t = k // 3, k % 3
            cols = pl.ds(pl.multiple_of(t * 384, 128), 384)
            up = dot(h2[chunk, :], wt[3 * s + 1, :, cols], NN)
            grad = dot(mlpg[chunk, :], wt[3 * s + 2, cols, :], NT)
            square = up * up
            th = jnp.tanh(GELU_ONE * (up + GELU_TWO * up * square))
            half_one = 0.5 * (1.0 + th)
            act = up * half_one
            slope = half_one + 0.5 * up * (1.0 - th * th) * (GELU_ONE * (1.0 + 3.0 * GELU_TWO * square))
            big[rows_at(GROUP * s + OWN * cc, OWN), cols] = act.astype(bf16)
            big[rows_at(2 * GROUP + GROUP * s + OWN * cc, OWN), cols] = (grad * slope).astype(bf16)
            return carry

        lax.fori_loop(0, 6, units, 0)

        def inputs_back(t, carry):
            cols = pl.ds(pl.multiple_of(t * 384, 128), 384)
            part = dot(big[rows_at(2 * GROUP + OWN * cc, OWN), :], wt[1, cols, :], NT)
            part += dot(big[rows_at(3 * GROUP + OWN * cc, OWN), :], wt[4, cols, :], NT)
            seco[chunk, cols] = part.astype(bf16)
            return carry

        lax.fori_loop(0, 3, inputs_back, 0)
        send(("sec", i), seco.at[chunk], secr.at[chunk], narrow_to(1))

        def down(t, carry):
            cols = pl.ds(pl.multiple_of(t * 384, 128), 384)
            part = dot(big[rows_at(OWN * cc, OWN), :], wt[2, :, cols], NN)
            part += dot(big[rows_at(GROUP + OWN * cc, OWN), :], wt[5, :, cols], NN)
            mlpp[cc, :, cols] = part.astype(bf16)
            return carry

        lax.fori_loop(0, 3, down, 0)

    send(("mlp",), mlpp.at[1 - low], mlpr, narrow_to(1))
    sent(("ag",))

    def kept(mask):
        return rows_at(block_of(mask) * BLK, BLK)

    def axes(m):
        return (2, 4) if m in (0, 4, 2) else (4, 2)

    def rs_core(m):
        for i, mask in enumerate((0, 2, 4, 6)):
            send(("rs", m, "c", i), wt.at[m, kept(mask ^ 1)], crecv.at[m, pl.ds(i * BLK, BLK)], wide_to(1))

    def add_into(m, mask, ref, at):
        def body(t, carry):
            r = rows_at(block_of(mask) * BLK + t * 16, 16)
            wt[m, r, :] = (
                wt[m, r, :].astype(f32) + ref[m, rows_at(at + t * 16, 16), :].astype(f32)
            ).astype(bf16)
            return carry

        lax.fori_loop(0, BLK // 16, body, 0)

    def rs_one(m):
        first, second = axes(m)
        for i, mask in enumerate((0, 2, 4, 6)):
            recv(("rs", m, "c", i), crecv.at[m, pl.ds(i * BLK, BLK)])
        for mask in (first, 6, 0, second):
            add_into(m, mask, crecv, mask // 2 * BLK)
        for i, mask in enumerate((0, second)):
            send(("rs", m, "f", i), wt.at[m, kept(mask ^ first)], frecv.at[m, pl.ds(i * BLK, BLK)], wide_to(first))

    def rs_two(m):
        first, second = axes(m)
        for i, mask in enumerate((0, second)):
            recv(("rs", m, "f", i), frecv.at[m, pl.ds(i * BLK, BLK)])
            add_into(m, mask, frecv, i * BLK)
        send(("rs", m, "s"), wt.at[m, kept(second)], srecv.at[m], wide_to(second))

    def rs_three(m):
        recv(("rs", m, "s"), srecv.at[m])
        add_into(m, 0, srecv, 0)
        if m >= 3:
            send(("rs", m, "z"), wt.at[m, kept(0)], zrecv.at[m - 3], narrow_to(2))

    outs = []

    def rs_four(m):
        recv(("rs", m + 3, "z"), zrecv.at[m])

        def body(t, carry):
            r = rows_at(t * 16, 16)
            mine = wt[m, rows_at(block_of(0) * BLK + t * 16, 16), :].astype(f32)
            total = mine + zrecv[m, r, :].astype(f32)
            for i in range(3):
                facc[m, rows_at(i * BLK + t * 16, 16), :] = total[:, i * 384 : (i + 1) * 384]
            return carry

        lax.fori_loop(0, BLK // 16, body, 0)
        for i in range(3):
            outs.append(
                load(("out", m, i), facc.at[m, pl.ds(i * BLK, BLK)], gw_o.at[m, :, pl.ds(i * 384, 384)])
            )

    def down_grad(s):
        def body(t, carry):
            cols = pl.ds(pl.multiple_of(t * 128, 128), 128)
            part = dot(big[pl.ds(GROUP * s, GROUP), cols], mlpg[...], TN)
            wt[3 * s + 2, rows_at(t * 128, 128, 128), :] = part.astype(bf16)
            return carry

        lax.fori_loop(0, 9, body, 0)

    def up_grad(s):
        def body(t, carry):
            cols = pl.ds(pl.multiple_of(t * 128, 128), 128)
            part = dot(h2[:, cols], big[pl.ds(2 * GROUP + GROUP * s, GROUP), :], TN)
            wt[3 * s + 1, rows_at(t * 128, 128, 128), :] = part.astype(bf16)
            return carry

        lax.fori_loop(0, 9, body, 0)

    down_grad(1)
    rs_core(5)
    down_grad(0)
    rs_core(2)
    rs_one(5)
    up_grad(1)
    rs_core(4)
    rs_one(2)
    up_grad(0)
    rs_core(1)
    rs_one(4)

    msum[...] = jnp.zeros((2, 6, D), f32)
    for i in range(2):
        cc = order(i)
        chunk = rows_at(OWN * cc, OWN)
        recv(("sec", i), secr.at[chunk])

        def parts(t):
            r = rows_at(OWN * cc + t * 32, 32, 32)
            ra = rows_at(off + OWN * cc + t * 32, 32, 32)
            block = 4 * high + 2 * cc + t // 4
            branch = attp[r, :].astype(f32) + attr[r, :].astype(f32)
            gate = mod_row(2, block)
            normal, scale = norm_parts(tok[ra, :].astype(f32) + gate * branch)
            grad = seco[r, :].astype(f32) + secr[r, :].astype(f32)
            mid = og[r, :].astype(f32) + norm_back(normal, scale, grad * (1.0 + mod_row(4, block)))
            attg[ra, :] = (gate * mid).astype(bf16)
            return branch, normal, grad, mid

        @pl.when(cc == low)
        def _():
            def body(t, carry):
                branch, normal, grad, mid = parts(t)
                mgrad[rows_at(t * 32, 32, 32), :] = mid
                at = t // 4
                for k, v in ((2, mid * branch), (3, grad), (4, grad * normal)):
                    msum[at, k : k + 1, :] += jnp.sum(v, axis=0, keepdims=True)
                return carry

            lax.fori_loop(0, OWN // 32, body, 0)

        @pl.when(cc != low)
        def _():
            def body(t, carry):
                parts(t)
                return carry

            lax.fori_loop(0, OWN // 32, body, 0)

        if i == 0:
            r = rows_at(off + 384 * (1 - high) + 64 * low, 64)
            send(("ahalo", 0), attg.at[r], attg.at[rows_at(halo_there + 64 * low, 64)], narrow_to(2))
            rs_one(1)
            rs_two(5)
            rs_two(2)
            r = rows_at(halo_at + 64 * low, 64)
            recv(("ahalo", 0), attg.at[r])
            send(("ahalo", 1), attg.at[r], attg.at[r], narrow_to(1))

    recv(("ahalo", 1), attg.at[rows_at(halo_at + 64 * (1 - low), 64)])
    rs_two(4)

    recv(("mlp",), mlpr)

    def mix(t, carry):
        r = rows_at(OWN * low + t * 32, 32, 32)
        ra = rows_at(own_at + t * 32, 32, 32)
        rr = rows_at(t * 32, 32, 32)
        block = 4 * high + 2 * low + t // 4
        branch = attp[r, :].astype(f32) + attr[r, :].astype(f32)
        middle = tok[ra, :].astype(f32) + mod_row(2, block) * branch
        mlp = mlpp[low, rr, :].astype(f32) + mlpr[rr, :].astype(f32)
        mlpr[rr, :] = (middle + mod_row(5, block) * mlp).astype(bf16)
        msum[t // 4, 5:6, :] += jnp.sum(og[r, :].astype(f32) * mlp, axis=0, keepdims=True)
        return carry

    lax.fori_loop(0, OWN // 32, mix, 0)
    outs.append(load("mixed", mlpr, mixed_o))

    def attend_back(s, j, k0, count):
        r = rows_at(j * SEG, SEG, SEG)
        keys = slice(k0 * SEG, (k0 + count) * SEG)
        bias = key_bias(j, k0, count)
        out = [jnp.zeros((SEG, 128), f32) for _ in range(3)]
        for hd, (a, width) in enumerate(WINDOWS):
            mask = head_mask(hd, SEG)
            cols = slice(a, a + width)
            q = jnp.where(mask, qkv[s, 0, r, cols].astype(f32), 0.0).astype(bf16)
            hg = jnp.where(mask, hgrad[r, cols].astype(f32), 0.0).astype(bf16)
            scores = dot(qkv[s, 1, keys, cols], q, NT) * FACTOR
            scores = jnp.concatenate(
                [scores[i * SEG : (i + 1) * SEG, :] + bias[i] for i in range(count)], axis=0
            )
            prob = jnp.exp(scores - lse_t[s, hd : hd + 1, r])
            prob_grad = dot(qkv[s, 2, keys, cols], hg, NT)
            inner = jnp.sum(prob * prob_grad, axis=0, keepdims=True)
            score_grad = (prob * (prob_grad - inner)).astype(bf16)
            facc[1, keys, cols] += dot(score_grad, q, NN)
            facc[2, keys, cols] += dot(prob.astype(bf16), hg, NN)
            res = jnp.where(mask, dot(score_grad, qkv[s, 1, keys, cols], TN), 0.0)
            for i in range(width // 128):
                out[a // 128 + i] += res[:, i * 128 : (i + 1) * 128]
        for i in range(3):
            facc[0, r, i * 128 : (i + 1) * 128] = out[i]

    def pack(s):
        lane = lax.broadcasted_iota(jnp.int32, (64, 384), 1)

        def body(t, carry):
            ra = rows_at(off + t * 64, 64, 64)
            rg = rows_at(GROUP * s + t * 64, 64, 64)
            q = jnp.where(lane < QUARTER, facc[0, ra, :] * FACTOR, 0.0)
            k = pltpu.roll(jnp.where(lane < QUARTER, facc[1, ra, :] * FACTOR, 0.0), 32, 1)
            v = pltpu.roll(jnp.where(lane < QUARTER, facc[2, ra, :], 0.0), 64, 1)
            hd = pltpu.roll(heads[s, ra, :].astype(f32), 96, 1)
            tiles = [
                q[:, 0:128],
                q[:, 128:256],
                q[:, 256:384] + k[:, 0:128],
                k[:, 128:256],
                k[:, 256:384] + v[:, 0:128],
                v[:, 128:256],
                v[:, 256:384],
            ]
            for i, tile in enumerate(tiles):
                big[rg, i * 128 : (i + 1) * 128] = tile.astype(bf16)
            heads[s, ra, :] = hd.astype(bf16)
            return carry

        lax.fori_loop(0, GROUP // 64, body, 0)

    for s in range(2):
        hgrad[:, 0:QUARTER] = dot(attg[...], wt[3 * s, 3 * QUARTER : D, :], NT).astype(bf16)
        facc[...] = jnp.zeros((3, ATT, 384), f32)
        for_blocks(functools.partial(attend_back, s))
        pack(s)
        if s == 0:
            rs_two(1)
            rs_three(5)
            rs_three(2)

    def first_back(half, at):
        def body(t, carry):
            cols = pl.ds(pl.multiple_of(t * 384, 128), 384)
            part = dot(big[rows_at(OWN * half, OWN), 0 : 3 * QUARTER], wt[0, 0 : 3 * QUARTER, cols], NN)
            part += dot(big[rows_at(GROUP + OWN * half, OWN), 0 : 3 * QUARTER], wt[3, 0 : 3 * QUARTER, cols], NN)
            big[pl.ds(2 * GROUP + at, OWN), cols] = part.astype(bf16)
            return carry

        lax.fori_loop(0, 3, body, 0)

    first_back(1 - low, 0)
    send(("first",), big.at[pl.ds(2 * GROUP, OWN)], firstr, narrow_to(1))

    def attn_grad(s):
        def body(t, carry):
            cols = pl.ds(pl.multiple_of(t * 128, 128), 128)
            rg = rows_at(off, GROUP)
            part = dot(h1[rg, cols], big[pl.ds(GROUP * s, GROUP), 0:896], TN)
            proj = dot(attg[rg, cols], heads[s, rg, :], TN)
            r = rows_at(t * 128, 128, 128)
            wt[3 * s, r, 0:768] = part[:, 0:768].astype(bf16)
            wt[3 * s, r, 768:896] = (part[:, 768:896] + proj[:, 0:128]).astype(bf16)
            wt[3 * s, r, 896:D] = proj[:, 128:384].astype(bf16)
            return carry

        lax.fori_loop(0, 9, body, 0)

    first_back(low, OWN)
    attn_grad(1)
    rs_core(3)
    attn_grad(0)
    rs_core(0)
    rs_one(3)
    rs_one(0)
    rs_three(4)
    rs_three(1)

    recv(("first",), firstr)

    def tokens_back(t, carry):
        ra = rows_at(own_at + t * 32, 32, 32)
        rr = rows_at(t * 32, 32, 32)
        block = 4 * high + 2 * low + t // 4
        normal, scale = norm_parts(tok[ra, :].astype(f32))
        grad = big[rows_at(2 * GROUP + OWN + t * 32, 32, 32), :].astype(f32) + firstr[rr, :].astype(f32)
        res = mgrad[rr, :] + norm_back(normal, scale, grad * (1.0 + mod_row(1, block)))
        firstr[rr, :] = res.astype(bf16)
        for k, v in ((0, grad), (1, grad * normal)):
            msum[t // 4, k : k + 1, :] += jnp.sum(v, axis=0, keepdims=True)
        return carry

    lax.fori_loop(0, OWN // 32, tokens_back, 0)
    outs.append(load("tg", firstr, tg_o))

    sent(("mod",))
    row = lax.broadcasted_iota(jnp.int32, (8, D), 0)
    lane = lax.broadcasted_iota(jnp.int32, (8, ATT), 1)
    for k in range(6):
        total = jnp.zeros((8, D), f32)
        for i in range(2):
            slot = seg[SEG * (4 * high + 2 * low + i)]
            total += jnp.where((row == slot) & (row < 4), msum[i, k : k + 1, :], 0.0)
        modrecv[2 * k] = jnp.where(lane < HALF, total[:, 0:ATT], 0.0)
        modrecv[2 * k + 1] = jnp.where(lane < HALF, pltpu.roll(total[:, 512:D], HALF, 1), 0.0)
    for mask in (1, 2, 3):
        m = narrow_to(mask)[1]
        send(("mg", mask), modrecv.at[pl.ds(3 * m, 3)], mgr.at[mask - 1], narrow_to(mask))
    rs_two(3)
    rs_two(0)
    for mask in (1, 2, 3):
        recv(("mg", mask), mgr.at[mask - 1])
    total = modrecv[pl.ds(3 * n, 3)] + mgr[0] + mgr[1] + mgr[2]
    mall[b] = total.astype(bf16).astype(f32)
    if gather_wide:
        for mask in range(1, 8):
            send(("mall", mask), mall.at[b], mall.at[b], wide_to(mask))
    rs_three(3)
    rs_three(0)
    rs_four(1)
    rs_four(2)
    if gather_wide:
        for mask in range(1, 8):
            recv(("silu", mask), silu_all.at[block_of(mask)])
            recv(("mall", mask), mall.at[block_of(mask)])
        pick_row = lax.broadcasted_iota(jnp.int32, (BLK, D), 0) + b * BLK
        pick_col = lax.broadcasted_iota(jnp.int32, (BLK, D), 1)
        pick = jnp.where(pick_row == pick_col, 1.0, 0.0).astype(bf16)
        left = dot(pick, silu_all[...].reshape(64, D).astype(bf16), NT).astype(bf16)
        for i in range(3):
            right = mall[:, i].reshape(64, ATT)
            wada_o[i] = dot(left, right.astype(bf16), NN)
            bada_o[i : i + 1, :] = jnp.sum(right, axis=0, keepdims=True)
    mod_o[...] = mall[b]
    rs_four(0)
    for copy in outs:
        copy.wait()
    sent(())


def shards(N, tokens, condition, segment, w_ada, b_ada, w_qkv, w_proj, w_up, w_down, out_grad):
    step = N // 8
    gather_wide = N == 8
    anywhere = pl.BlockSpec(memory_space=pl.ANY)
    vmem = pl.BlockSpec(memory_space=pltpu.VMEM)
    smem = pl.BlockSpec(memory_space=pltpu.SMEM)
    shape = jax.ShapeDtypeStruct
    V = pltpu.VMEM
    out = pl.pallas_call(
        functools.partial(kernel, gather_wide, step),
        name="block",
        out_shape=(
            shape((OWN, D), bf16),
            shape((OWN, D), bf16),
            shape((3, BLK, D), f32),
            shape((3, 8, ATT), f32),
            shape((3, BLK, ATT), f32),
            shape((3, ATT), f32),
        ),
        in_specs=[smem, vmem, vmem] + [anywhere] * 7,
        out_specs=(anywhere, anywhere, anywhere, vmem, vmem, vmem),
        scratch_shapes=[
            V((6, D, D), bf16),
            V((6, 4 * BLK, D), bf16),
            V((6, 2 * BLK, D), bf16),
            V((6, BLK, D), bf16),
            V((3, BLK, D), bf16),
            V((ATT, D), bf16),
            V((GROUP, D), bf16),
            V((ATT, D), bf16),
            V((2, 3, ATT, 384), bf16),
            V((2, ATT, 384), bf16),
            V((2, 8, ATT), f32),
            V((GROUP, D), bf16),
            V((GROUP, D), bf16),
            V((GROUP, D), bf16),
            V((GROUP, D), bf16),
            V((4 * GROUP, D), bf16),
            V((2, OWN, D), bf16),
            V((OWN, D), bf16),
            V((GROUP, D), bf16),
            V((GROUP, D), bf16),
            V((OWN, D), f32),
            V((ATT, D), bf16),
            V((ATT, 384), bf16),
            V((3, ATT, 384), f32),
            V((OWN, D), bf16),
            V((6, 8, D), f32),
            V((12, 8, ATT), f32),
            V((8, 8, D), f32),
            V((2, 6, D), f32),
            V((3, 3, 8, ATT), f32),
            V((8, 3, 8, ATT), f32),
            V((16, D), f32),
            pltpu.SemaphoreType.DMA((SEMS,)),
            pltpu.SemaphoreType.DMA((SEMS,)),
            pltpu.SemaphoreType.DMA((24,)),
        ],
        compiler_params=pltpu.CompilerParams(
            collective_id=0, has_side_effects=True, vmem_limit_bytes=63 * 2**20
        ),
    )(
        segment,
        condition,
        b_ada.astype(f32).reshape(3, HALF),
        tokens,
        out_grad,
        w_ada.T,
        w_qkv.transpose(1, 2, 0).reshape(3 * QUARTER, D),
        w_proj.T,
        w_up,
        w_down,
    )
    mixed, tokens_grad, grads, mod, wada, bada = out
    if gather_wide:
        w_ada_grad = jnp.concatenate([wada[i, :, :HALF] for i in range(3)], axis=1)
        b_all = jnp.concatenate([bada[i, :HALF] for i in range(3)], axis=0)
    else:
        silu_low = jax.nn.silu(condition.astype(f32)).astype(bf16)
        mod_grad = jnp.concatenate([mod[i, :4, :HALF] for i in range(3)], axis=1).astype(bf16)
        silu_wide = lax.all_gather(silu_low, "wide", axis=0, tiled=True)
        mod_wide = lax.all_gather(mod_grad, "wide", axis=0, tiled=True)
        rows = D // N
        left = lax.dynamic_slice_in_dim(silu_wide, lax.axis_index("wide") * rows, rows, axis=1)
        w_ada_grad = jnp.einsum("id,ic->dc", left, mod_wide, preferred_element_type=f32)
        b_all = jnp.sum(mod_wide.astype(f32), axis=0)
        groups = [[i * step + r for r in range(step)] for i in range(8)]
        grads = lax.psum_scatter(grads, "wide", scatter_dimension=1, axis_index_groups=groups, tiled=True)
    part = b_all.shape[0] // N
    b_ada_grad = lax.dynamic_slice_in_dim(b_all, lax.axis_index("wide") * part, part)
    rows = D // N
    w_qkv_grad = grads[0, :, : 3 * QUARTER].reshape(rows, 3, QUARTER)
    return (
        mixed,
        tokens_grad,
        w_ada_grad,
        b_ada_grad,
        w_qkv_grad,
        grads[0, :, 3 * QUARTER :],
        grads[1],
        grads[2],
    )


def solution(mesh):
    placed = (
        P(("wide", "narrow"), None),
        P("wide", None),
        P("wide"),
        P(None, "narrow"),
        P("narrow"),
        P(None, None, "narrow"),
        P(None, "narrow"),
        P(None, "narrow"),
        P("narrow", None),
        P(("wide", "narrow"), None),
    )
    return jax.shard_map(
        functools.partial(shards, mesh.shape["wide"]),
        mesh=mesh,
        in_specs=placed,
        out_specs=(
            P(("wide", "narrow"), None),
            P(("wide", "narrow"), None),
            P("wide", "narrow"),
            P(("narrow", "wide")),
            P("wide", None, "narrow"),
            P("wide", "narrow"),
            P("wide", "narrow"),
            P(("narrow", "wide"), None),
        ),
        check_vma=False,
    )
```

time: 900 us -> 277 us (0.31)
  waiting for transfers between devices: 660 us -> 0 us
  Pallas kernels: 0 us -> 264 us
  matrix products: 120 us -> 0 us
  other arithmetic: 35 us -> 0 us
  blocking collectives: 28.8 us -> 0 us
  local copies, waits for them, and re-layouts: 33 us -> 12.4 us
  between operations: 15.5 us -> 0.68 us
    reduce_scatter x9 -> x0, waiting for transfers between devices: 459 us -> none  [the longest x1 74.7 us: shards(): lax.psum_scatter(w_ada_grad, 'wide', scatter_dimension=0, tiled=True)]
    pallas_call x0 -> x1, Pallas kernels: none -> 264 us  [shards(): pl.pallas_call(functools.partial(kernel, gather_wide, step), name='block'...]
    all_gather x4 -> x0, waiting for transfers between devices: 194 us -> none  [the longest x1 51.5 us: shards(): lax.all_gather(hidden_one.astype(jnp.bfloat16), 'narrow', axis=0, tiled=T...]
    dot_general x30 -> x0, matrix products: 120 us -> none  [the longest x1 10.3 us: shards(): up_values = jnp.dot(second_all, w_up, preferred_element_type=jnp.float32)]
    reduce_sum x10 -> x0, other arithmetic: 16.8 us -> none  [the longest x4 8.66 us: normalize(): centred = inputs - jnp.mean(inputs, axis=-1, keepdims=True)]
    all_gather x1 -> x0, blocking collectives: 15.1 us -> none  [shards(): modulation = lax.all_gather(mod_part, 'narrow', axis=1, tiled=True)]
    unnamed x95 -> x9, local copies, waits for them, and re-layouts: 16.4 us -> 2.52 us
    unnamed x1 -> x0, blocking collectives: 13.7 us -> none
  transfers between devices with their start and end apart: 14 -> 0, of which waited for: 14 -> 0; matrix products, arithmetic and copies ran while one was open for 6% -> 0% of each run, Pallas kernels for 0% -> 0%
where the time goes in v1:
time: 277 us
  Pallas kernels  264 us (95%)
  local copies, waits for them, and re-layouts  12.4 us (4%)
    pallas_call x1, Pallas kernels, shards(): pl.pallas_call(functools.partial(kernel, gather_wide, step), name='block'...  264 us

profile of v1, /device:TPU:0, one launch (start us, length us, event | category | flops | bytes accessed | tf_op | source)
XLA Modules:
  0.0 277.0 jit_solution(8883113767930160304)
XLA Ops:
  0.6 1.4 reshape.28.bada
  2.0 263.9 %block.1 = (bf16[256,1152]{1,0:T(8,128)(2,1)}, bf16[256,1152]{1,0:T(8,128)(2,1)}, f32[3,144,1152]{2,1,0:T(8,128)}, f32[3,8,640]{2,1,0:T(8,128)}, f32[3,144,640]{2,1,0:T(8,128)}, /*index=5*/f32[3,640]{1,0:T(4,128)}) custom-call(s32[1024]{0:T(1024)} %seg.1, bf16[4,1152]{1,0:T(4,128)(2,1)} %cond.1, f32[3,576]{1,0:T(4,128)} %reshape.28.bada, ...), custom_call_target="tpu_custom_call" | custom-call | tf_op jit(solution)/shard_map/block/pallas_call | solution.py:749
  265.9 0.8 slice_reduce_fusion
  266.8 0.1 concatenate.7
  266.8 0.6 dynamic_slice.3
  267.5 1.7 slice_bitcast_fusion.5
  269.2 1.1 slice.36
  270.3 2.4 slice_bitcast_fusion
  272.7 0.0 copy-start
  272.7 0.4 reshape_squeeze.3
  273.2 0.9 copy.19
  274.1 0.0 copy-done
  274.1 0.0 copy-start.2
  274.1 0.1 slice_bitcast_fusion.2
  274.1 0.0 copy-start.1
  274.1 1.2 concatenate.6
  275.3 0.0 copy-done.2
  275.3 0.8 copy.22
  276.1 0.0 copy-done.1
  276.1 0.8 copy.23
Async XLA Ops:
  272.7 1.3 copy-start
  274.1 1.3 copy-start.2
  274.1 2.0 copy-start.1

commit v2 on v1

v2 whole, which is shorter than its diff:
```python
import functools
import math

import jax
import jax.numpy as jnp
from jax import lax
from jax.experimental import pallas as pl
from jax.experimental.pallas import tpu as pltpu
from jax.sharding import PartitionSpec as P

D = 1152
HEAD = 72
HEADS_LOCAL = 4
QUARTER = 288
HALF = 576
BLK = 144
SUB_A = 80
SEG = 128
OWN = 256
GROUP = 512
ATT = 640
NEG = -1e30
EPS = 1e-6
FACTOR = HEAD ** -0.5
GELU_ONE = math.sqrt(2.0 / math.pi)
GELU_TWO = 0.044715

f32, bf16 = jnp.float32, jnp.bfloat16
MESH = pl.DeviceIdType.MESH
NN = (((1,), (0,)), ((), ()))
NT = (((1,), (1,)), ((), ()))
TN = (((0,), (0,)), ((), ()))
PAIRS = ((0, (0, 1)), (128, (2, 3)))


def dot(a, b, dims):
    return lax.dot_general(a, b, dims, preferred_element_type=f32)


def rows_at(start, size, align=16):
    return pl.ds(pl.multiple_of(start, align), size)


def mean_row(v):
    return jnp.sum(v, axis=-1, keepdims=True) * (1.0 / D)


def norm_parts(v):
    centred = v - mean_row(v)
    scale = lax.rsqrt(mean_row(centred * centred) + EPS)
    return centred * scale, scale


def norm_back(normal, scale, e):
    return scale * (e - mean_row(e) - normal * mean_row(e * normal))


class Names:
    def __init__(self):
        self.ids = {}

    def __call__(self, *name):
        return self.ids.setdefault(name, len(self.ids))


SEMS = 122


def mark(name):
    pass


def kernel(
    gather_wide, step,
    seg, cond, bada, tok_h, og_h, wada_h, wqkv_h, wproj_h, wup_h, wdown_h,
    mixed_o, tg_o, gown_o, gfar_o, mall_o, silu_o,
    wt, crecv, frecv, srecv, zrecv, tok, og, h1, qkv, heads, lse_t, attp, attr, h2, mlpg, big,
    mlpp, mlpr, seco, secr, mgrad, attg, hgrad, facc, keys_t, dq_t, firstr, modblk, modrecv, silu_all, msum, mgs, mgr, mall, silu16, credit,
    ssem, rsem, lsem,
):
    w = lax.axis_index("wide")
    n = lax.axis_index("narrow")
    b = w // step
    bits = (b % 2, (b // 2) % 2, b // 4)
    low, high = n % 2, n // 2

    def narrow_to(mask):
        m = n
        if mask & 1:
            m = m + 1 - 2 * low
        if mask & 2:
            m = m + 2 - 4 * high
        return (w, m)

    def wide_to(mask):
        m = w
        for k in range(3):
            if mask & (1 << k):
                m = m + step * (1 << k) * (1 - 2 * bits[k])
        return (m, n)

    def block_of(mask):
        m = b
        for k in range(3):
            if mask & (1 << k):
                m = m + (1 << k) * (1 - 2 * bits[k])
        return m

    names = Names()

    def remote(name, src, dst, dev):
        k = names(*name)
        return pltpu.make_async_remote_copy(
            src_ref=src, dst_ref=dst, send_sem=ssem.at[k], recv_sem=rsem.at[k], device_id=dev, device_id_type=MESH
        )

    sends = {}

    def send(name, src, dst, dev):
        copy = remote(name, src, dst, dev)
        copy.start()
        sends[name] = copy

    def recv(name, landing):
        remote(name, landing, landing, narrow_to(1)).wait_recv()

    def sent(prefix):
        for name in [s for s in sends if s[: len(prefix)] == prefix]:
            sends.pop(name).wait_send()

    locals_ = Names()

    def load(name, src, dst):
        copy = pltpu.make_async_copy(src, dst, lsem.at[locals_(name)])
        copy.start()
        return copy

    off = 128 * high
    own_at = off + OWN * low
    other_at = off + OWN * (1 - low)
    halo_at = GROUP * (1 - high)
    halo_there = GROUP * high

    mark("loads")
    load_m = load("m", wada_h, big.at[pl.ds(0, 3 * HALF)])
    load_a = load("a", wqkv_h, wt.at[0, pl.ds(0, 3 * QUARTER)])
    load_b = load("b", wproj_h, wt.at[0, pl.ds(3 * QUARTER, QUARTER)])
    load_t = load("t", tok_h, tok.at[rows_at(own_at, OWN)])
    load_u = load("u", wup_h, wt.at[1])
    load_d = load("d", wdown_h, wt.at[2])
    load_g = load("g", og_h, og.at[rows_at(OWN * low, OWN)])
    barrier = pltpu.get_barrier_semaphore()
    partners = [narrow_to(m) for m in (1, 2, 3)] + [wide_to(m) for m in (range(1, 8) if gather_wide else (1, 2, 4))]
    for dev in partners:
        pl.semaphore_signal(barrier, inc=1, device_id=dev, device_id_type=MESH)

    c = cond[...].astype(f32)
    silu = (c / (1.0 + jnp.exp(-c))).astype(bf16).astype(f32)
    silu16[...] = jnp.zeros((16, D), f32)
    for i in range(3):
        silu16[4 * i : 4 * i + 4, :] = silu
    silu_low = silu16[...].astype(bf16)
    silu_all[b] = silu_low
    mark("wait_wada")
    load_m.wait()
    mark("mod_dots")
    third = lax.broadcasted_iota(jnp.int32, (16, HALF), 0) // 4
    part = jnp.zeros((16, HALF), f32)
    for i in range(3):
        value = dot(silu_low, big[HALF * i : HALF * (i + 1), :], NT) + bada[i : i + 1, :]
        part = jnp.where(third == i, value, part)
    modrecv[n, :, 0:HALF] = part
    modrecv[n, :, HALF:ATT] = jnp.zeros((16, ATT - HALF), f32)
    modblk[...] = jnp.zeros((6, 8, D), f32)
    mark("barrier")
    pl.semaphore_wait(barrier, len(partners))

    def allow(i):
        pl.semaphore_signal(credit.at[i], inc=1, device_id=narrow_to(2), device_id_type=MESH)

    def allowed(i):
        pl.semaphore_wait(credit.at[i], 1)

    def block_rows(mask, part=None):
        base = block_of(mask) * BLK
        if part is None:
            return rows_at(base, BLK)
        return rows_at(base, SUB_A) if part == 0 else rows_at(base + SUB_A, BLK - SUB_A)

    def ag_z(m):
        r = block_rows(0)
        send(("ag", m, "z"), wt.at[m, r], wt.at[3 + m, r], narrow_to(2))

    def ag_pass(m, name, mask, axis, part=None):
        r = block_rows(mask, part)
        send(("ag", m) + name, wt.at[3 + m, r], wt.at[3 + m, r], wide_to(axis))

    def ag_take(m, name, mask, part=None):
        recv(("ag", m) + name, wt.at[3 + m, block_rows(mask, part)])

    def ag_one(m):
        ag_take(m, ("z",), 0)
        ag_pass(m, ("x",), 0, 2)
        ag_pass(m, ("y",), 0, 4)
        ag_pass(m, ("c", 0), 0, 1)

    def ag_two(m):
        ag_take(m, ("x",), 2)
        ag_pass(m, ("xy",), 2, 4, 0)
        ag_take(m, ("y",), 4)
        ag_pass(m, ("yx",), 4, 2, 1)
        ag_pass(m, ("c", 2), 2, 1)
        ag_pass(m, ("c", 4), 4, 1)

    def ag_three(m):
        ag_take(m, ("xy",), 6, 0)
        ag_take(m, ("yx",), 6, 1)
        ag_pass(m, ("c", 6), 6, 1)

    def ag_end(m):
        for mask in (0, 2, 4, 6):
            ag_take(m, ("c", mask), mask ^ 1)

    mark("first_sends")
    for mask in (1, 2, 3):
        send(("mod", mask), modrecv.at[n], modrecv.at[n], narrow_to(mask))
    send(("tok",), tok_h, tok.at[rows_at(own_at, OWN)], narrow_to(1))
    halo_first = remote(
        ("halo", 0), tok_h.at[rows_at(128 * (1 - high), SEG)], tok.at[rows_at(halo_there, SEG)], narrow_to(2)
    )
    halo_second = remote(
        ("halo", 1), tok.at[rows_at(halo_at, SEG)], tok.at[rows_at(halo_at, SEG)], narrow_to(1)
    )
    halo_source = low != high

    @pl.when(halo_source)
    def _():
        halo_first.start()

    load_a.wait()
    load_b.wait()
    ag_z(0)
    mark("wait_mod")
    for mask in (1, 2, 3):
        m = narrow_to(mask)[1]
        recv(("mod", mask), modrecv.at[m])
    for k in range(6):
        halves = [modrecv[i // 3, i % 3 * 4 : i % 3 * 4 + 4, :] for i in (2 * k, 2 * k + 1)]
        first, second = halves[0], pltpu.roll(halves[1], 64, 1)
        modblk[k, 0:4, 0:512] = first[:, 0:512]
        modblk[k, 0:4, 512:640] = first[:, 512:640] + second[:, 0:128]
        modblk[k, 0:4, 640:D] = second[:, 128:640]

    def mod_row(k, shard_block):
        return modblk[k, pl.ds(seg[shard_block * SEG], 1), :]

    def first_norm(base, size):
        def body(t, carry):
            r = rows_at(base + t * 32, 32, 32)
            block = 3 * high + (base + t * 32) // SEG
            normal, _ = norm_parts(tok[r, :].astype(f32))
            h1[r, :] = (normal * (1.0 + mod_row(1, block)) + mod_row(0, block)).astype(bf16)
            return carry

        lax.fori_loop(0, size // 32, body, 0)

    mark("norm_own")
    load_t.wait()
    first_norm(own_at, OWN)
    mark("wait_halo")

    @pl.when(jnp.logical_not(halo_source))
    def _():
        halo_first.wait_recv()
        halo_second.start()

    mark("wait_tok")
    recv(("tok",), tok.at[rows_at(other_at, OWN)])
    allow(0)
    mark("norm_other")
    first_norm(other_at, OWN)
    mark("wait_ag_one_0")
    ag_one(0)
    mark("wait_halo_two")

    @pl.when(halo_source)
    def _():
        halo_second.wait_recv()
        halo_first.wait_send()

    mark("norm_halo")
    first_norm(halo_at, SEG)

    @pl.when(jnp.logical_not(halo_source))
    def _():
        halo_second.wait_send()

    def project(s):
        def body(i, carry):
            qkv[s, i] = dot(h1[...], wt[3 * s, rows_at(QUARTER * i, 384), :], NT).astype(bf16)
            return carry

        lax.fori_loop(0, 3, body, 0)

    def key_bias(j, k0, count):
        mine = seg[SEG * (j + 3 * high)]
        return [jnp.where(seg[SEG * (k0 + i + 3 * high)] == mine, 0.0, NEG) for i in range(count)]

    lane_pair = lax.broadcasted_iota(jnp.int32, (SEG, 256), 1)
    pair_masks = [
        [(lane_pair >= HEAD * hd - a) & (lane_pair < HEAD * (hd + 1) - a) for hd in hds] for a, hds in PAIRS
    ]

    def stacked(value, masks):
        value = value.astype(f32)
        return jnp.concatenate([jnp.where(m, value, 0.0).astype(bf16) for m in masks], axis=0)

    def attend(s, j, k0, count):
        r = rows_at(j * SEG, SEG, SEG)
        keys = slice(k0 * SEG, (k0 + count) * SEG)
        bias = key_bias(j, k0, count)
        out = [jnp.zeros((SEG, 128), f32) for _ in range(3)]
        lse = jnp.zeros((SEG, 128), f32)
        lane = lax.broadcasted_iota(jnp.int32, (SEG, 128), 1)
        for (a, hds), masks in zip(PAIRS, pair_masks):
            cols = slice(a, a + 256)
            scores = dot(stacked(qkv[s, 0, r, cols], masks), qkv[s, 1, keys, cols], NT) * FACTOR
            scores = jnp.concatenate(
                [scores[:, i * SEG : (i + 1) * SEG] + bias[i] for i in range(count)], axis=1
            )
            top = jnp.max(scores, axis=1, keepdims=True)
            weights = jnp.exp(scores - top)
            total = jnp.sum(weights, axis=1, keepdims=True)
            prob = (weights * (1.0 / total)).astype(bf16)
            res = dot(prob, qkv[s, 2, keys, cols], NN)
            log_total = top + jnp.log(total)
            for i, hd in enumerate(hds):
                part = jnp.where(masks[i], res[i * SEG : (i + 1) * SEG, :], 0.0)
                out[a // 128] += part[:, 0:128]
                out[a // 128 + 1] += part[:, 128:256]
                lse = jnp.where(lane == hd, log_total[i * SEG : (i + 1) * SEG, :], lse)
        for i in range(3):
            heads[s, r, i * 128 : (i + 1) * 128] = out[i].astype(bf16)
        lse_t[s, :, r] = lse.T[0:8, :]

    def for_blocks(fn, between=()):
        fn(0, 0, 2)
        for hook in between[0:1]:
            hook()
        fn(1, 0, 5)
        for hook in between[1:2]:
            hook()

        def body(j, carry):
            fn(j, 1, 4)
            return carry

        lax.fori_loop(2, 5, body, 0)

    mark("project_own")
    project(0)
    load_u.wait()
    load_d.wait()
    allowed(0)
    ag_z(1)
    ag_z(2)
    mark("wait_ag_two_0")
    ag_two(0)
    mark("attend_own")
    for_blocks(functools.partial(attend, 0), (lambda: None, lambda: ag_three(0)))
    load_g.wait()
    send(("og",), og_h, og.at[rows_at(OWN * low, OWN)], narrow_to(1))
    mark("wait_ag_end_0")
    ag_end(0)
    ag_one(1)
    mark("project_opp")
    project(1)
    mark("wait_ag_one_2")
    ag_one(2)
    mark("attend_opp")
    for_blocks(functools.partial(attend, 1), (lambda: None, lambda: ag_two(1)))
    mark("proj")
    def order(i):
        return 1 - high if i == 0 else high

    if gather_wide:
        for mask in range(1, 8):
            send(("silu", mask), silu_all.at[b], silu_all.at[b], wide_to(mask))
    for i in range(2):
        cc = order(i)
        src = rows_at(off + OWN * cc, OWN)
        dst = rows_at(OWN * cc, OWN)

        def body(t, carry):
            cols = pl.ds(pl.multiple_of(t * 384, 128), 384)
            part = dot(heads[0, src, 0:QUARTER], wt[0, 3 * QUARTER : D, cols], NN)
            part += dot(heads[1, src, 0:QUARTER], wt[3, 3 * QUARTER : D, cols], NN)
            attp[dst, cols] = part.astype(bf16)
            return carry

        lax.fori_loop(0, 3, body, 0)
        if i == 0:
            send(("att", i), attp.at[dst], attr.at[dst], narrow_to(1))

    mark("wait_ag_two_2")
    ag_two(2)
    ag_three(1)
    mark("wait_ag_three_2")
    ag_three(2)
    mark("wait_og")
    recv(("og",), og.at[rows_at(OWN * (1 - low), OWN)])

    mark("ffn")
    for i in range(2):
        cc = order(i)
        chunk = rows_at(OWN * cc, OWN)
        mark("wait_att")
        recv(("att", i), attr.at[chunk])
        if i == 0:
            dst = rows_at(OWN * order(1), OWN)
            send(("att", 1), attp.at[dst], attr.at[dst], narrow_to(1))

        mark("second_norm")
        def second_norm(t, carry):
            r = rows_at(OWN * cc + t * 32, 32, 32)
            ra = rows_at(off + OWN * cc + t * 32, 32, 32)
            block = 4 * high + 2 * cc + t // 4
            branch = attp[r, :].astype(f32) + attr[r, :].astype(f32)
            middle = tok[ra, :].astype(f32) + mod_row(2, block) * branch
            normal, _ = norm_parts(middle)
            h2[r, :] = (normal * (1.0 + mod_row(4, block)) + mod_row(3, block)).astype(bf16)
            mlpg[r, :] = (mod_row(5, block) * og[r, :].astype(f32)).astype(bf16)
            return carry

        lax.fori_loop(0, OWN // 32, second_norm, 0)
        if i == 0:
            mark("wait_ag_end")
            ag_end(1)
            ag_end(2)

        mark("units")
        def units(k, carry):
            s, t = k // 3, k % 3
            cols = pl.ds(pl.multiple_of(t * 384, 128), 384)
            up = dot(h2[chunk, :], wt[3 * s + 1, :, cols], NN)
            grad = dot(mlpg[chunk, :], wt[3 * s + 2, cols, :], NT)
            square = up * up
            th = jnp.tanh(GELU_ONE * (up + GELU_TWO * up * square))
            half_one = 0.5 * (1.0 + th)
            act = up * half_one
            slope = half_one + 0.5 * up * (1.0 - th * th) * (GELU_ONE * (1.0 + 3.0 * GELU_TWO * square))
            big[rows_at(GROUP * s + OWN * cc, OWN), cols] = act.astype(bf16)
            big[rows_at(2 * GROUP + GROUP * s + OWN * cc, OWN), cols] = (grad * slope).astype(bf16)
            return carry

        lax.fori_loop(0, 6, units, 0)

        mark("inputs_back")
        def inputs_back(t, carry):
            cols = pl.ds(pl.multiple_of(t * 384, 128), 384)
            part = dot(big[rows_at(2 * GROUP + OWN * cc, OWN), :], wt[1, cols, :], NT)
            part += dot(big[rows_at(3 * GROUP + OWN * cc, OWN), :], wt[4, cols, :], NT)
            seco[chunk, cols] = part.astype(bf16)
            return carry

        lax.fori_loop(0, 3, inputs_back, 0)
        send(("sec", i), seco.at[chunk], secr.at[chunk], narrow_to(1))

    mark("drain_ag")
    sent(("ag",))

    def kept(mask):
        return rows_at(block_of(mask) * BLK, BLK)

    def pieces(m):
        return ((pl.ds(0, 640), 2, 4), (pl.ds(640, 512), 4, 2))

    def rs_core(m):
        for i, mask in enumerate((0, 2, 4, 6)):
            send(("rs", m, "c", i), wt.at[m, kept(mask ^ 1)], crecv.at[m, pl.ds(i * BLK, BLK)], wide_to(1))

    def add_into(m, mask, ref, at, cols):
        def body(t, carry):
            r = rows_at(block_of(mask) * BLK + t * 16, 16)
            wt[m, r, cols] = (
                wt[m, r, cols].astype(f32) + ref[m, rows_at(at + t * 16, 16), cols].astype(f32)
            ).astype(bf16)
            return carry

        lax.fori_loop(0, BLK // 16, body, 0)

    def rs_one(m):
        for i, mask in enumerate((0, 2, 4, 6)):
            recv(("rs", m, "c", i), crecv.at[m, pl.ds(i * BLK, BLK)])
        for p, (cols, first, second) in enumerate(pieces(m)):
            for mask in (first, 6):
                add_into(m, mask, crecv, mask // 2 * BLK, cols)
            for i, mask in enumerate((0, second)):
                send(
                    ("rs", m, "f", p, i), wt.at[m, kept(mask ^ first), cols], frecv.at[m, pl.ds(i * BLK, BLK), cols],
                    wide_to(first),
                )
        for p, (cols, first, second) in enumerate(pieces(m)):
            for mask in (0, second):
                add_into(m, mask, crecv, mask // 2 * BLK, cols)

    def rs_two(m):
        for p, (cols, first, second) in enumerate(pieces(m)):
            recv(("rs", m, "f", p, 1), frecv.at[m, pl.ds(BLK, BLK), cols])
            add_into(m, second, frecv, BLK, cols)
            send(("rs", m, "s", p), wt.at[m, kept(second), cols], srecv.at[m, :, cols], wide_to(second))
        for p, (cols, first, second) in enumerate(pieces(m)):
            recv(("rs", m, "f", p, 0), frecv.at[m, pl.ds(0, BLK), cols])
            add_into(m, 0, frecv, 0, cols)

    outs = []

    def rs_three(m):
        for p, (cols, _, _) in enumerate(pieces(m)):
            recv(("rs", m, "s", p), srecv.at[m, :, cols])
            add_into(m, 0, srecv, 0, cols)
        if m >= 3:
            send(("rs", m, "z"), wt.at[m, kept(0)], zrecv.at[m - 3], narrow_to(2))
        else:
            outs.append(load(("own", m), wt.at[m, kept(0)], gown_o.at[m]))

    def rs_four(m):
        recv(("rs", m + 3, "z"), zrecv.at[m])
        outs.append(load(("far", m), zrecv.at[m], gfar_o.at[m]))

    def down(t, carry):
        cols = pl.ds(pl.multiple_of(t * 384, 128), 384)
        part = dot(big[0:GROUP, :], wt[2, :, cols], NN)
        part += dot(big[GROUP : 2 * GROUP, :], wt[5, :, cols], NN)
        mlpp[:, :, cols] = part.astype(bf16).reshape(2, OWN, 384)
        return carry

    def down_grad(s):
        def body(t, carry):
            cols = pl.ds(pl.multiple_of(t * 128, 128), 128)
            part = dot(big[pl.ds(GROUP * s, GROUP), cols], mlpg[...], TN)
            wt[3 * s + 2, rows_at(t * 128, 128, 128), :] = part.astype(bf16)
            return carry

        lax.fori_loop(0, 9, body, 0)

    def up_grad(s):
        def body(t, carry):
            cols = pl.ds(pl.multiple_of(t * 128, 128), 128)
            part = dot(h2[:, cols], big[pl.ds(2 * GROUP + GROUP * s, GROUP), :], TN)
            wt[3 * s + 1, rows_at(t * 128, 128, 128), :] = part.astype(bf16)
            return carry

        lax.fori_loop(0, 9, body, 0)

    mark("up_grad_1")
    up_grad(1)
    rs_core(4)
    msum[...] = jnp.zeros((2, 6, D), f32)
    for i in range(2):
        cc = order(i)
        chunk = rows_at(OWN * cc, OWN)
        mark("wait_sec")
        recv(("sec", i), secr.at[chunk])
        mark("second_norm_back")

        def parts(t):
            r = rows_at(OWN * cc + t * 32, 32, 32)
            ra = rows_at(off + OWN * cc + t * 32, 32, 32)
            block = 4 * high + 2 * cc + t // 4
            branch = attp[r, :].astype(f32) + attr[r, :].astype(f32)
            gate = mod_row(2, block)
            normal, scale = norm_parts(tok[ra, :].astype(f32) + gate * branch)
            grad = seco[r, :].astype(f32) + secr[r, :].astype(f32)
            mid = og[r, :].astype(f32) + norm_back(normal, scale, grad * (1.0 + mod_row(4, block)))
            attg[ra, :] = (gate * mid).astype(bf16)
            return branch, normal, grad, mid

        @pl.when(cc == low)
        def _():
            def body(t, carry):
                branch, normal, grad, mid = parts(t)
                mgrad[rows_at(t * 32, 32, 32), :] = mid
                at = t // 4
                for k, v in ((2, mid * branch), (3, grad), (4, grad * normal)):
                    msum[at, k : k + 1, :] += jnp.sum(v, axis=0, keepdims=True)
                return carry

            lax.fori_loop(0, OWN // 32, body, 0)

        @pl.when(cc != low)
        def _():
            def body(t, carry):
                parts(t)
                return carry

            lax.fori_loop(0, OWN // 32, body, 0)

        if i == 0:
            r = rows_at(off + 384 * (1 - high) + 64 * low, 64)
            send(("ahalo", 0), attg.at[r], attg.at[rows_at(halo_there + 64 * low, 64)], narrow_to(2))
            mark("rs_one_4")
            rs_one(4)
            mark("down")
            lax.fori_loop(0, 3, down, 0)
            mark("down_grad_1")
            down_grad(1)
            rs_core(5)
            mark("wait_halo_back")
            r = rows_at(halo_at + 64 * low, 64)
            recv(("ahalo", 0), attg.at[r])
            send(("ahalo", 1), attg.at[r], attg.at[r], narrow_to(1))

    mark("wait_halo_back_two")
    recv(("ahalo", 1), attg.at[rows_at(halo_at + 64 * (1 - low), 64)])
    send(("mlp",), mlpp.at[1 - low], mlpr, narrow_to(1))

    def mix(t, carry):
        r = rows_at(OWN * low + t * 32, 32, 32)
        ra = rows_at(own_at + t * 32, 32, 32)
        rr = rows_at(t * 32, 32, 32)
        block = 4 * high + 2 * low + t // 4
        branch = attp[r, :].astype(f32) + attr[r, :].astype(f32)
        middle = tok[ra, :].astype(f32) + mod_row(2, block) * branch
        mlp = mlpp[low, rr, :].astype(f32) + mlpr[rr, :].astype(f32)
        mlpr[rr, :] = (middle + mod_row(5, block) * mlp).astype(bf16)
        msum[t // 4, 5:6, :] += jnp.sum(og[r, :].astype(f32) * mlp, axis=0, keepdims=True)
        return carry

    def attend_back(s, j, k0, count):
        r = rows_at(j * SEG, SEG, SEG)
        keys = slice(k0 * SEG, (k0 + count) * SEG)
        bias = key_bias(j, k0, count)
        row = lax.broadcasted_iota(jnp.int32, (256, SEG), 0)
        for (a, hds), masks in zip(PAIRS, pair_masks):
            cols = slice(a, a + 256)
            q = stacked(qkv[s, 0, r, cols], masks)
            hg = stacked(hgrad[r, cols], masks)
            top = jnp.concatenate([lse_t[s, hd : hd + 1, r] for hd in hds], axis=1)
            scores = dot(qkv[s, 1, keys, cols], q, NT) * FACTOR
            prob = jnp.exp(
                jnp.concatenate(
                    [scores[i * SEG : (i + 1) * SEG, :] - (top - bias[i]) for i in range(count)], axis=0
                )
            )
            prob_grad = dot(qkv[s, 2, keys, cols], hg, NT)
            inner = jnp.sum(prob * prob_grad, axis=0, keepdims=True)
            score_grad = (prob * (prob_grad - inner)).astype(bf16)
            facc[0, keys, cols] += dot(score_grad, q, NN)
            facc[1, keys, cols] += dot(prob.astype(bf16), hg, NN)
            res = dot(keys_t[a : a + 256, keys], score_grad, NN)
            total = jnp.zeros((256, SEG), f32)
            for i, hd in enumerate(hds):
                mine = (row >= HEAD * hd - a) & (row < HEAD * (hd + 1) - a)
                total += jnp.where(mine, res[:, i * SEG : (i + 1) * SEG], 0.0)
            dq_t[a : a + 256, r] += total

    def pack(s):
        lane = lax.broadcasted_iota(jnp.int32, (128, 384), 1)

        def body(t, carry):
            ra = rows_at(off + t * 128, 128, 128)
            rg = rows_at(GROUP * s + t * 128, 128, 128)
            q = jnp.where(lane < QUARTER, dq_t[:, ra].T * FACTOR, 0.0)
            k = pltpu.roll(jnp.where(lane < QUARTER, facc[0, ra, :] * FACTOR, 0.0), 32, 1)
            v = pltpu.roll(jnp.where(lane < QUARTER, facc[1, ra, :], 0.0), 64, 1)
            hd = pltpu.roll(heads[s, ra, :].astype(f32), 96, 1)
            tiles = [
                q[:, 0:128],
                q[:, 128:256],
                q[:, 256:384] + k[:, 0:128],
                k[:, 128:256],
                k[:, 256:384] + v[:, 0:128],
                v[:, 128:256],
                v[:, 256:384],
            ]
            for i, tile in enumerate(tiles):
                big[rg, i * 128 : (i + 1) * 128] = tile.astype(bf16)
            heads[s, ra, :] = hd.astype(bf16)
            return carry

        lax.fori_loop(0, GROUP // 128, body, 0)

    def first_far(t, carry):
        half, cols = t // 3, pl.ds(pl.multiple_of(t % 3 * 384, 128), 384)
        part = dot(big[rows_at(GROUP + OWN * half, OWN), 0 : 3 * QUARTER], wt[3, 0 : 3 * QUARTER, cols], NN)
        high_part = part.astype(bf16)
        secr[rows_at(OWN * half, OWN), cols] = high_part
        mlpg[rows_at(OWN * half, OWN), cols] = (part - high_part.astype(f32)).astype(bf16)
        return carry

    def first_back(half, at):
        def body(t, carry):
            cols = pl.ds(pl.multiple_of(t * 384, 128), 384)
            part = dot(big[rows_at(OWN * half, OWN), 0 : 3 * QUARTER], wt[0, 0 : 3 * QUARTER, cols], NN)
            part += secr[rows_at(OWN * half, OWN), cols].astype(f32)
            part += mlpg[rows_at(OWN * half, OWN), cols].astype(f32)
            seco[pl.ds(at, OWN), cols] = part.astype(bf16)
            return carry

        lax.fori_loop(0, 3, body, 0)

    def attn_grad(s):
        def body(t, carry):
            cols = pl.ds(pl.multiple_of(t * 128, 128), 128)
            rg = rows_at(off, GROUP)
            part = dot(h1[rg, cols], big[pl.ds(GROUP * s, GROUP), 0:896], TN)
            proj = dot(attg[rg, cols], heads[s, rg, :], TN)
            r = rows_at(t * 128, 128, 128)
            wt[3 * s, r, 0:768] = part[:, 0:768].astype(bf16)
            wt[3 * s, r, 768:896] = (part[:, 768:896] + proj[:, 0:128]).astype(bf16)
            wt[3 * s, r, 896:D] = proj[:, 128:384].astype(bf16)
            return carry

        lax.fori_loop(0, 9, body, 0)

    def heads_back(s, between):
        mark("heads_grad")
        hgrad[:, 0:QUARTER] = dot(attg[...], wt[3 * s, 3 * QUARTER : D, :], NT).astype(bf16)
        facc[...] = jnp.zeros((2, ATT, 384), f32)
        dq_t[...] = jnp.zeros((384, ATT), f32)
        for i in range(5):
            keys_t[:, i * 128 : (i + 1) * 128] = qkv[s, 1, i * 128 : (i + 1) * 128, :].T
        mark("attend_back")
        for_blocks(functools.partial(attend_back, s), between)
        mark("pack")
        pack(s)

    mark("rs_one_5")
    rs_one(5)
    mark("down_grad_0")
    down_grad(0)
    rs_core(2)
    heads_back(1, (lambda: rs_two(4), lambda: rs_one(2)))
    mark("first_far")
    lax.fori_loop(0, 6, first_far, 0)
    mark("attn_grad_1")
    attn_grad(1)
    rs_core(3)
    mark("rs_three_4")
    rs_three(4)
    rs_two(5)
    mark("up_grad_0")
    up_grad(0)
    rs_core(1)
    mark("rs_one_3")
    rs_one(3)
    rs_two(2)
    heads_back(0, (lambda: rs_three(5), lambda: rs_one(1)))
    sent(("sec",))
    mark("first_back")
    first_back(1 - low, 0)
    send(("first",), seco.at[pl.ds(0, OWN)], firstr, narrow_to(1))
    mark("first_back_own")
    first_back(low, OWN)
    mark("rs_two_3")
    rs_two(3)
    mark("attn_grad_0")
    attn_grad(0)
    rs_core(0)
    mark("rs_three_21")
    rs_three(2)
    rs_two(1)
    mark("rs_one_0")
    rs_one(0)
    mark("wait_mlp")
    recv(("mlp",), mlpr)
    mark("mix")
    lax.fori_loop(0, OWN // 32, mix, 0)
    outs.append(load("mixed", mlpr, mixed_o))

    mark("wait_first")
    recv(("first",), firstr)
    allow(1)

    mark("tokens_back")
    def tokens_back(t, carry):
        ra = rows_at(own_at + t * 32, 32, 32)
        rr = rows_at(t * 32, 32, 32)
        block = 4 * high + 2 * low + t // 4
        normal, scale = norm_parts(tok[ra, :].astype(f32))
        grad = seco[rows_at(OWN + t * 32, 32, 32), :].astype(f32) + firstr[rr, :].astype(f32)
        res = mgrad[rr, :] + norm_back(normal, scale, grad * (1.0 + mod_row(1, block)))
        firstr[rr, :] = res.astype(bf16)
        for k, v in ((0, grad), (1, grad * normal)):
            msum[t // 4, k : k + 1, :] += jnp.sum(v, axis=0, keepdims=True)
        return carry

    lax.fori_loop(0, OWN // 32, tokens_back, 0)
    outs.append(load("tg", firstr, tg_o))

    mark("modgrad")
    sent(("mod",))
    row = lax.broadcasted_iota(jnp.int32, (8, D), 0)
    lane = lax.broadcasted_iota(jnp.int32, (8, ATT), 1)
    for k in range(6):
        total = jnp.zeros((8, D), f32)
        for i in range(2):
            slot = seg[SEG * (4 * high + 2 * low + i)]
            total += jnp.where((row == slot) & (row < 4), msum[i, k : k + 1, :], 0.0)
        for i, value in ((2 * k, total[:, 0:ATT]), (2 * k + 1, pltpu.roll(total[:, 512:D], HALF, 1))):
            modrecv[i // 3, i % 3 * 4 : i % 3 * 4 + 4, :] = jnp.where(lane < HALF, value, 0.0)[0:4, :]
    for i in range(4):
        modrecv[i, 12:16, :] = jnp.zeros((4, ATT), f32)
        mgs[i] = modrecv[i].astype(bf16)
    for mask in (1, 2, 3):
        m = narrow_to(mask)[1]
        send(("mg", mask), mgs.at[m], mgr.at[mask - 1], narrow_to(mask))
    mark("rs_three_3")
    allowed(1)
    rs_three(3)
    rs_three(1)
    mark("rs_two_0")
    rs_two(0)
    rs_four(2)
    rs_four(1)
    mark("wait_mg")
    for mask in (1, 2, 3):
        recv(("mg", mask), mgr.at[mask - 1])
    total = modrecv[n] + mgr[0].astype(f32) + mgr[1].astype(f32) + mgr[2].astype(f32)
    mall[b] = total.astype(bf16)
    if gather_wide:
        for mask in range(1, 8):
            send(("mall", mask), mall.at[b], mall.at[b], wide_to(mask))
    mark("rs_three_0")
    rs_three(0)
    mark("rs_four_0")
    rs_four(0)
    mark("wait_mall")
    if gather_wide:
        for mask in range(1, 8):
            recv(("silu", mask), silu_all.at[block_of(mask)])
            recv(("mall", mask), mall.at[block_of(mask)])
    outs.append(load("mall", mall, mall_o))
    outs.append(load("silu", silu_all, silu_o))
    mark("drain")
    for copy in outs:
        copy.wait()
    sent(())
    mark(None)


def finish(
    step, mixed_h, tg_h, gown_h, gfar_h, mall_h, silu_h,
    mixed_o, tg_o, wada_o, bada_o, gqkv_o, gproj_o, gup_o, gdown_o,
    gown, gfar, mall, silu, mixed, tg, wada, sums, bada, gqkv, gproj, gffn, sem,
):
    ids = Names()

    def move(src, dst):
        copy = pltpu.make_async_copy(src, dst, sem.at[ids(len(ids.ids))])
        copy.start()
        return copy

    ins = [move(mall_h, mall), move(silu_h, silu), move(gown_h, gown), move(gfar_h, gfar)]
    outs = []
    rows = [move(mixed_h, mixed), move(tg_h, tg)]
    rows[0].wait()
    outs.append(move(mixed, mixed_o))
    rows[1].wait()
    outs.append(move(tg, tg_o))
    b = lax.axis_index("wide") // step
    ins[0].wait()
    ins[1].wait()
    pick_row = lax.broadcasted_iota(jnp.int32, (BLK, D), 0) + b * BLK
    pick_col = lax.broadcasted_iota(jnp.int32, (BLK, D), 1)
    pick = jnp.where(pick_row == pick_col, 1.0, 0.0).astype(bf16)
    left = dot(pick, silu[...].reshape(128, D), NT).astype(bf16)
    third = lax.broadcasted_iota(jnp.int32, (BLK, 128), 1) % 16 // 4
    right = mall[...].reshape(128, ATT)
    for i in range(3):
        part = dot(jnp.where(third == i, left, 0), right, NN)
        total = dot(jnp.where(third[0:8] == i, 1.0, 0.0).astype(bf16), right, NN)
        if i == 1:
            part, total = pltpu.roll(part, 64, 1), pltpu.roll(total, 64, 1)
            wada[:, 512:640] += part[:, 0:128]
            wada[:, 640:D] = part[:, 128:640]
            sums[:, 512:640] += total[:, 0:128]
            sums[:, 640:D] = total[:, 128:640]
        else:
            at = i * HALF
            wada[:, at : at + HALF] = part[:, 0:HALF]
            sums[:, at : at + ATT] = total
            if i == 0:
                wada[:, HALF:640] = jnp.zeros((BLK, 64), f32)
    place = lax.axis_index("wide")
    bada[...] = pltpu.roll(sums[...], 14 * 128 - place * QUARTER // 4 * 3, 1)[:, 0:256]
    outs.append(move(wada, wada_o))
    outs.append(move(bada, bada_o))
    ins[2].wait()
    ins[3].wait()
    for m in range(3):
        total = gown[m].astype(f32) + gfar[m].astype(f32)
        if m == 0:
            gqkv[0] = total[:, 0:QUARTER]
            gqkv[1] = pltpu.roll(total[:, 256:640], 352, 1)[:, 0:QUARTER]
            gqkv[2] = pltpu.roll(total[:, 512:896], 320, 1)[:, 0:QUARTER]
            gproj[...] = pltpu.roll(total[:, 768:D], 288, 1)[:, 0:QUARTER]
            outs.append(move(gqkv, gqkv_o))
            outs.append(move(gproj, gproj_o))
        else:
            gffn[m - 1] = total
            outs.append(move(gffn.at[m - 1], (gup_o, gdown_o)[m - 1]))
    for copy in outs:
        copy.wait()


def shards(N, tokens, condition, segment, w_ada, b_ada, w_qkv, w_proj, w_up, w_down, out_grad):
    step = N // 8
    gather_wide = N == 8
    anywhere = pl.BlockSpec(memory_space=pl.ANY)
    hbm = pl.BlockSpec(memory_space=pltpu.HBM)
    vmem = pl.BlockSpec(memory_space=pltpu.VMEM)
    smem = pl.BlockSpec(memory_space=pltpu.SMEM)
    shape = jax.ShapeDtypeStruct
    V = pltpu.VMEM
    out = pl.pallas_call(
        functools.partial(kernel, gather_wide, step),
        name="block",
        out_shape=(
            shape((OWN, D), bf16),
            shape((OWN, D), bf16),
            shape((3, BLK, D), bf16),
            shape((3, BLK, D), bf16),
            shape((8, 16, ATT), bf16),
            shape((8, 16, D), bf16),
        ),
        in_specs=[smem, vmem, vmem] + [anywhere] * 7,
        out_specs=(anywhere,) * 6,
        scratch_shapes=[
            V((6, D, D), bf16),
            V((6, 4 * BLK, D), bf16),
            V((6, 2 * BLK, D), bf16),
            V((6, BLK, D), bf16),
            V((3, BLK, D), bf16),
            V((ATT, D), bf16),
            V((GROUP, D), bf16),
            V((ATT, D), bf16),
            V((2, 3, ATT, 384), bf16),
            V((2, ATT, 384), bf16),
            V((2, 8, ATT), f32),
            V((GROUP, D), bf16),
            V((GROUP, D), bf16),
            V((GROUP, D), bf16),
            V((GROUP, D), bf16),
            V((4 * GROUP, D), bf16),
            V((2, OWN, D), bf16),
            V((OWN, D), bf16),
            V((GROUP, D), bf16),
            V((GROUP, D), bf16),
            V((OWN, D), f32),
            V((ATT, D), bf16),
            V((ATT, 384), bf16),
            V((2, ATT, 384), f32),
            V((384, ATT), bf16),
            V((384, ATT), f32),
            V((OWN, D), bf16),
            V((6, 8, D), f32),
            V((4, 16, ATT), f32),
            V((8, 16, D), bf16),
            V((2, 6, D), f32),
            V((4, 16, ATT), bf16),
            V((3, 16, ATT), bf16),
            V((8, 16, ATT), bf16),
            V((16, D), f32),
            pltpu.SemaphoreType.REGULAR((2,)),
            pltpu.SemaphoreType.DMA((SEMS,)),
            pltpu.SemaphoreType.DMA((SEMS,)),
            pltpu.SemaphoreType.DMA((17,)),
        ],
        compiler_params=pltpu.CompilerParams(
            collective_id=0, has_side_effects=True, vmem_limit_bytes=63 * 2**20
        ),
    )(
        segment,
        condition,
        b_ada.astype(f32).reshape(3, HALF),
        tokens,
        out_grad,
        w_ada.T,
        w_qkv.transpose(1, 2, 0).reshape(3 * QUARTER, D),
        w_proj.T,
        w_up,
        w_down,
    )
    mixed, tokens_grad, gown, gfar, mall, silu = out
    mixed, tokens_grad, wada, bada, gqkv, gproj, gup, gdown = pl.pallas_call(
        functools.partial(finish, step),
        name="finish",
        out_shape=(
            shape((OWN, D), bf16),
            shape((OWN, D), bf16),
            shape((BLK, 3 * HALF), f32),
            shape((8, 256), f32),
            shape((3, BLK, QUARTER), f32),
            shape((BLK, QUARTER), f32),
            shape((BLK, D), f32),
            shape((BLK, D), f32),
        ),
        in_specs=[hbm] * 6,
        out_specs=(hbm,) * 8,
        scratch_shapes=[
            V((3, BLK, D), bf16),
            V((3, BLK, D), bf16),
            V((8, 16, ATT), bf16),
            V((8, 16, D), bf16),
            V((OWN, D), bf16),
            V((OWN, D), bf16),
            V((BLK, 3 * HALF), f32),
            V((8, 14 * 128), f32),
            V((8, 256), f32),
            V((3, BLK, QUARTER), f32),
            V((BLK, QUARTER), f32),
            V((2, BLK, D), f32),
            pltpu.SemaphoreType.DMA((16,)),
        ],
        compiler_params=pltpu.CompilerParams(vmem_limit_bytes=63 * 2**20),
    )(mixed, tokens_grad, gown, gfar, mall, silu)
    gqkv = gqkv.transpose(1, 0, 2)
    place = lax.axis_index("wide")
    if gather_wide:
        w_ada_grad, b_ada_grad = wada, bada[0, : 3 * HALF // N]
    else:
        silu_low = jax.nn.silu(condition.astype(f32)).astype(bf16)
        mine = lax.dynamic_index_in_dim(mall, place // step, keepdims=False)
        mod_grad = jnp.concatenate([mine[4 * i : 4 * i + 4, :HALF] for i in range(3)], axis=1)
        silu_wide = lax.all_gather(silu_low, "wide", axis=0, tiled=True)
        mod_wide = lax.all_gather(mod_grad, "wide", axis=0, tiled=True)
        left = lax.dynamic_slice_in_dim(silu_wide, place * (D // N), D // N, axis=1)
        w_ada_grad = jnp.einsum("id,ic->dc", left, mod_wide, preferred_element_type=f32)
        b_all = jnp.sum(mod_wide.astype(f32), axis=0)
        groups = [[i * step + r for r in range(step)] for i in range(8)]
        gqkv, gproj, gup, gdown = (
            lax.psum_scatter(g, "wide", scatter_dimension=0, axis_index_groups=groups, tiled=True)
            for g in (gqkv, gproj, gup, gdown)
        )
        part = b_all.shape[0] // N
        b_ada_grad = lax.dynamic_slice_in_dim(b_all, place * part, part)
    return (mixed, tokens_grad, w_ada_grad, b_ada_grad, gqkv, gproj, gup, gdown)


def solution(mesh):
    placed = (
        P(("wide", "narrow"), None),
        P("wide", None),
        P("wide"),
        P(None, "narrow"),
        P("narrow"),
        P(None, None, "narrow"),
        P(None, "narrow"),
        P(None, "narrow"),
        P("narrow", None),
        P(("wide", "narrow"), None),
    )
    return jax.shard_map(
        functools.partial(shards, mesh.shape["wide"]),
        mesh=mesh,
        in_specs=placed,
        out_specs=(
            P(("wide", "narrow"), None),
            P(("wide", "narrow"), None),
            P("wide", "narrow"),
            P(("narrow", "wide")),
            P("wide", None, "narrow"),
            P("wide", "narrow"),
            P("wide", "narrow"),
            P(("narrow", "wide"), None),
        ),
        check_vma=False,
    )
```

time: 277 us -> 226 us (0.82)
  Pallas kernels: 264 us -> 223 us
  local copies, waits for them, and re-layouts: 12.4 us -> 2.63 us
    pallas_call x1, Pallas kernels: 264 us -> 218 us  [shards(): pl.pallas_call(functools.partial(kernel, gather_wide, step), name='block'...]
    pallas_call x0 -> x1, Pallas kernels: none -> 4.7 us  [shards(): pl.pallas_call(functools.partial(finish, step), name='finish', out_shape=...]
    squeeze x3 -> x0, local copies, waits for them, and re-layouts: 4.25 us -> none  [the longest x1 2.44 us: shards(): grads[2]]
where the time goes in v2:
time: 226 us
  Pallas kernels  223 us (99%)
  local copies, waits for them, and re-layouts  2.63 us (1%)
    pallas_call x1, Pallas kernels, shards(): pl.pallas_call(functools.partial(kernel, gather_wide, step), name='block'...  218 us
    pallas_call x1, Pallas kernels, shards(): pl.pallas_call(functools.partial(finish, step), name='finish', out_shape=...  4.7 us

profile of v2, /device:TPU:0, one launch (start us, length us, event | category | flops | bytes accessed | tf_op | source)
XLA Modules:
  0.0 225.9 jit_solution(1268217692418643277)
XLA Ops:
  0.6 1.4 reshape.28.bada
  2.0 217.9 %block.1 = (bf16[256,1152]{1,0:T(8,128)(2,1)}, bf16[256,1152]{1,0:T(8,128)(2,1)}, bf16[3,144,1152]{2,1,0:T(8,128)(2,1)}, bf16[3,144,1152]{2,1,0:T(8,128)(2,1)}, ...) custom-call(s32[1024]{0:T(1024)} %seg.1, bf16[4,1152]{1,0:T(4,128)(2,1)} %cond.1, f32[3,576]{1,0:T(4,128)} %reshape.28.bada, ...), custom_call_target="tpu_custom_call" | custom-call | tf_op jit(solution)/shard_map/block/pallas_call | solution.py:917
  219.9 4.7 %finish.1 = (bf16[256,1152]{1,0:T(8,128)(2,1)}, bf16[256,1152]{1,0:T(8,128)(2,1)}, f32[144,1728]{1,0:T(8,128)}, f32[8,256]{1,0:T(8,128)}, f32[3,144,288]{2,1,0:T...) custom-call(bf16[256,1152]{1,0:T(8,128)(2,1)} %get-tuple-element.22.mixed_h, ...), custom_call_target="tpu_custom_call" | custom-call | tf_op jit(solution)/shard_map/finish/pallas_call | solution.py:987
  224.6 1.3 slice.3

commit v3 on v2

--- a/solution.py
+++ b/solution.py
@@ -55,6 +55,10 @@
     return scale * (e - mean_row(e) - normal * mean_row(e * normal))
 
 
+def by_eight(v):
+    return sum(v[i : i + 8, :] for i in range(0, v.shape[0], 8))
+
+
 class Names:
     def __init__(self):
         self.ids = {}
@@ -64,10 +68,6 @@
 
 
 SEMS = 122
-
-
-def mark(name):
-    pass
 
 
 def kernel(
@@ -75,7 +75,7 @@
     seg, cond, bada, tok_h, og_h, wada_h, wqkv_h, wproj_h, wup_h, wdown_h,
     mixed_o, tg_o, gown_o, gfar_o, mall_o, silu_o,
     wt, crecv, frecv, srecv, zrecv, tok, og, h1, qkv, heads, lse_t, attp, attr, h2, mlpg, big,
-    mlpp, mlpr, seco, secr, mgrad, attg, hgrad, facc, keys_t, dq_t, firstr, modblk, modrecv, silu_all, msum, mgs, mgr, mall, silu16, credit,
+    mlpp, mlpr, seco, secr, mgrad, attg, hgrad, facc, keys_t, dq_t, firstr, modblk, modrecv, silu_all, msum, mgs, mgr, mall, silu16,
     ssem, rsem, lsem,
 ):
     w = lax.axis_index("wide")
@@ -141,7 +141,6 @@
     halo_at = GROUP * (1 - high)
     halo_there = GROUP * high
 
-    mark("loads")
     load_m = load("m", wada_h, big.at[pl.ds(0, 3 * HALF)])
     load_a = load("a", wqkv_h, wt.at[0, pl.ds(0, 3 * QUARTER)])
     load_b = load("b", wproj_h, wt.at[0, pl.ds(3 * QUARTER, QUARTER)])
@@ -161,9 +160,7 @@
         silu16[4 * i : 4 * i + 4, :] = silu
     silu_low = silu16[...].astype(bf16)
     silu_all[b] = silu_low
-    mark("wait_wada")
     load_m.wait()
-    mark("mod_dots")
     third = lax.broadcasted_iota(jnp.int32, (16, HALF), 0) // 4
     part = jnp.zeros((16, HALF), f32)
     for i in range(3):
@@ -172,14 +169,7 @@
     modrecv[n, :, 0:HALF] = part
     modrecv[n, :, HALF:ATT] = jnp.zeros((16, ATT - HALF), f32)
     modblk[...] = jnp.zeros((6, 8, D), f32)
-    mark("barrier")
     pl.semaphore_wait(barrier, len(partners))
-
-    def allow(i):
-        pl.semaphore_signal(credit.at[i], inc=1, device_id=narrow_to(2), device_id_type=MESH)
-
-    def allowed(i):
-        pl.semaphore_wait(credit.at[i], 1)
 
     def block_rows(mask, part=None):
         base = block_of(mask) * BLK
@@ -221,7 +211,6 @@
         for mask in (0, 2, 4, 6):
             ag_take(m, ("c", mask), mask ^ 1)
 
-    mark("first_sends")
     for mask in (1, 2, 3):
         send(("mod", mask), modrecv.at[n], modrecv.at[n], narrow_to(mask))
     send(("tok",), tok_h, tok.at[rows_at(own_at, OWN)], narrow_to(1))
@@ -240,7 +229,6 @@
     load_a.wait()
     load_b.wait()
     ag_z(0)
-    mark("wait_mod")
     for mask in (1, 2, 3):
         m = narrow_to(mask)[1]
         recv(("mod", mask), modrecv.at[m])
@@ -264,31 +252,27 @@
 
         lax.fori_loop(0, size // 32, body, 0)
 
-    mark("norm_own")
     load_t.wait()
     first_norm(own_at, OWN)
-    mark("wait_halo")
 
     @pl.when(jnp.logical_not(halo_source))
     def _():
         halo_first.wait_recv()
         halo_second.start()
 
-    mark("wait_tok")
+    ag_one(0)
+    load_u.wait()
+    ag_z(1)
     recv(("tok",), tok.at[rows_at(other_at, OWN)])
-    allow(0)
-    mark("norm_other")
+    load_g.wait()
+    send(("og",), og_h, og.at[rows_at(OWN * low, OWN)], narrow_to(1))
     first_norm(other_at, OWN)
-    mark("wait_ag_one_0")
-    ag_one(0)
-    mark("wait_halo_two")
 
     @pl.when(halo_source)
     def _():
         halo_second.wait_recv()
         halo_first.wait_send()
 
-    mark("norm_halo")
     first_norm(halo_at, SEG)
 
     @pl.when(jnp.logical_not(halo_source))
@@ -357,29 +341,16 @@
 
         lax.fori_loop(2, 5, body, 0)
 
-    mark("project_own")
     project(0)
-    load_u.wait()
     load_d.wait()
-    allowed(0)
-    ag_z(1)
     ag_z(2)
-    mark("wait_ag_two_0")
     ag_two(0)
-    mark("attend_own")
     for_blocks(functools.partial(attend, 0), (lambda: None, lambda: ag_three(0)))
-    load_g.wait()
-    send(("og",), og_h, og.at[rows_at(OWN * low, OWN)], narrow_to(1))
-    mark("wait_ag_end_0")
+    ag_one(1)
     ag_end(0)
-    ag_one(1)
-    mark("project_opp")
     project(1)
-    mark("wait_ag_one_2")
-    ag_one(2)
-    mark("attend_opp")
-    for_blocks(functools.partial(attend, 1), (lambda: None, lambda: ag_two(1)))
-    mark("proj")
+    for_blocks(functools.partial(attend, 1))
+    ag_two(1)
     def order(i):
         return 1 - high if i == 0 else high
 
@@ -402,25 +373,18 @@
         if i == 0:
             send(("att", i), attp.at[dst], attr.at[dst], narrow_to(1))
 
-    mark("wait_ag_two_2")
-    ag_two(2)
     ag_three(1)
-    mark("wait_ag_three_2")
-    ag_three(2)
-    mark("wait_og")
+    ag_one(2)
     recv(("og",), og.at[rows_at(OWN * (1 - low), OWN)])
 
-    mark("ffn")
     for i in range(2):
         cc = order(i)
         chunk = rows_at(OWN * cc, OWN)
-        mark("wait_att")
         recv(("att", i), attr.at[chunk])
         if i == 0:
             dst = rows_at(OWN * order(1), OWN)
             send(("att", 1), attp.at[dst], attr.at[dst], narrow_to(1))
 
-        mark("second_norm")
         def second_norm(t, carry):
             r = rows_at(OWN * cc + t * 32, 32, 32)
             ra = rows_at(off + OWN * cc + t * 32, 32, 32)
@@ -434,11 +398,9 @@
 
         lax.fori_loop(0, OWN // 32, second_norm, 0)
         if i == 0:
-            mark("wait_ag_end")
+            ag_two(2)
             ag_end(1)
-            ag_end(2)
-
-        mark("units")
+
         def units(k, carry):
             s, t = k // 3, k % 3
             cols = pl.ds(pl.multiple_of(t * 384, 128), 384)
@@ -453,9 +415,12 @@
             big[rows_at(2 * GROUP + GROUP * s + OWN * cc, OWN), cols] = (grad * slope).astype(bf16)
             return carry
 
-        lax.fori_loop(0, 6, units, 0)
-
-        mark("inputs_back")
+        lax.fori_loop(0, 3, units, 0)
+        if i == 0:
+            ag_three(2)
+            ag_end(2)
+        lax.fori_loop(3, 6, units, 0)
+
         def inputs_back(t, carry):
             cols = pl.ds(pl.multiple_of(t * 384, 128), 384)
             part = dot(big[rows_at(2 * GROUP + OWN * cc, OWN), :], wt[1, cols, :], NT)
@@ -466,7 +431,6 @@
         lax.fori_loop(0, 3, inputs_back, 0)
         send(("sec", i), seco.at[chunk], secr.at[chunk], narrow_to(1))
 
-    mark("drain_ag")
     sent(("ag",))
 
     def kept(mask):
@@ -481,13 +445,11 @@
 
     def add_into(m, mask, ref, at, cols):
         def body(t, carry):
-            r = rows_at(block_of(mask) * BLK + t * 16, 16)
-            wt[m, r, cols] = (
-                wt[m, r, cols].astype(f32) + ref[m, rows_at(at + t * 16, 16), cols].astype(f32)
-            ).astype(bf16)
-            return carry
-
-        lax.fori_loop(0, BLK // 16, body, 0)
+            r = rows_at(block_of(mask) * BLK + t * 48, 48)
+            wt[m, r, cols] = wt[m, r, cols] + ref[m, rows_at(at + t * 48, 48), cols]
+            return carry
+
+        lax.fori_loop(0, BLK // 48, body, 0)
 
     def rs_one(m):
         for i, mask in enumerate((0, 2, 4, 6)):
@@ -535,34 +497,34 @@
         mlpp[:, :, cols] = part.astype(bf16).reshape(2, OWN, 384)
         return carry
 
+    def by_columns(fn, count, tail=None):
+        def body(t, carry):
+            fn(pl.ds(pl.multiple_of(t * 256, 128), 256))
+            return carry
+
+        lax.fori_loop(0, count, body, 0)
+        if tail is not None:
+            fn(pl.ds(tail, 128))
+
     def down_grad(s):
-        def body(t, carry):
-            cols = pl.ds(pl.multiple_of(t * 128, 128), 128)
-            part = dot(big[pl.ds(GROUP * s, GROUP), cols], mlpg[...], TN)
-            wt[3 * s + 2, rows_at(t * 128, 128, 128), :] = part.astype(bf16)
-            return carry
-
-        lax.fori_loop(0, 9, body, 0)
+        def tile(cols):
+            wt[3 * s + 2, :, cols] = dot(big[pl.ds(GROUP * s, GROUP), :], mlpg[:, cols], TN).astype(bf16)
+
+        by_columns(tile, 4, 1024)
 
     def up_grad(s):
-        def body(t, carry):
-            cols = pl.ds(pl.multiple_of(t * 128, 128), 128)
-            part = dot(h2[:, cols], big[pl.ds(2 * GROUP + GROUP * s, GROUP), :], TN)
-            wt[3 * s + 1, rows_at(t * 128, 128, 128), :] = part.astype(bf16)
-            return carry
-
-        lax.fori_loop(0, 9, body, 0)
-
-    mark("up_grad_1")
+        def tile(cols):
+            wt[3 * s + 1, :, cols] = dot(h2[...], big[pl.ds(2 * GROUP + GROUP * s, GROUP), cols], TN).astype(bf16)
+
+        by_columns(tile, 4, 1024)
+
     up_grad(1)
     rs_core(4)
-    msum[...] = jnp.zeros((2, 6, D), f32)
+    msum[...] = jnp.zeros((2, 6, 8, D), f32)
     for i in range(2):
         cc = order(i)
         chunk = rows_at(OWN * cc, OWN)
-        mark("wait_sec")
         recv(("sec", i), secr.at[chunk])
-        mark("second_norm_back")
 
         def parts(t):
             r = rows_at(OWN * cc + t * 32, 32, 32)
@@ -583,7 +545,7 @@
                 mgrad[rows_at(t * 32, 32, 32), :] = mid
                 at = t // 4
                 for k, v in ((2, mid * branch), (3, grad), (4, grad * normal)):
-                    msum[at, k : k + 1, :] += jnp.sum(v, axis=0, keepdims=True)
+                    msum[at, k] += by_eight(v)
                 return carry
 
             lax.fori_loop(0, OWN // 32, body, 0)
@@ -599,19 +561,18 @@
         if i == 0:
             r = rows_at(off + 384 * (1 - high) + 64 * low, 64)
             send(("ahalo", 0), attg.at[r], attg.at[rows_at(halo_there + 64 * low, 64)], narrow_to(2))
-            mark("rs_one_4")
             rs_one(4)
-            mark("down")
             lax.fori_loop(0, 3, down, 0)
-            mark("down_grad_1")
             down_grad(1)
             rs_core(5)
-            mark("wait_halo_back")
+            down_grad(0)
+            rs_core(2)
+            rs_two(4)
+            rs_one(5)
             r = rows_at(halo_at + 64 * low, 64)
             recv(("ahalo", 0), attg.at[r])
             send(("ahalo", 1), attg.at[r], attg.at[r], narrow_to(1))
 
-    mark("wait_halo_back_two")
     recv(("ahalo", 1), attg.at[rows_at(halo_at + 64 * (1 - low), 64)])
     send(("mlp",), mlpp.at[1 - low], mlpr, narrow_to(1))
 
@@ -624,7 +585,7 @@
         middle = tok[ra, :].astype(f32) + mod_row(2, block) * branch
         mlp = mlpp[low, rr, :].astype(f32) + mlpr[rr, :].astype(f32)
         mlpr[rr, :] = (middle + mod_row(5, block) * mlp).astype(bf16)
-        msum[t // 4, 5:6, :] += jnp.sum(og[r, :].astype(f32) * mlp, axis=0, keepdims=True)
+        msum[t // 4, 5] += by_eight(og[r, :].astype(f32) * mlp)
         return carry
 
     def attend_back(s, j, k0, count):
@@ -701,79 +662,54 @@
         lax.fori_loop(0, 3, body, 0)
 
     def attn_grad(s):
-        def body(t, carry):
-            cols = pl.ds(pl.multiple_of(t * 128, 128), 128)
-            rg = rows_at(off, GROUP)
-            part = dot(h1[rg, cols], big[pl.ds(GROUP * s, GROUP), 0:896], TN)
-            proj = dot(attg[rg, cols], heads[s, rg, :], TN)
-            r = rows_at(t * 128, 128, 128)
-            wt[3 * s, r, 0:768] = part[:, 0:768].astype(bf16)
-            wt[3 * s, r, 768:896] = (part[:, 768:896] + proj[:, 0:128]).astype(bf16)
-            wt[3 * s, r, 896:D] = proj[:, 128:384].astype(bf16)
-            return carry
-
-        lax.fori_loop(0, 9, body, 0)
+        rg = rows_at(off, GROUP)
+
+        def tile(cols):
+            wt[3 * s, :, cols] = dot(h1[rg, :], big[pl.ds(GROUP * s, GROUP), cols], TN).astype(bf16)
+
+        by_columns(tile, 3)
+        part = dot(h1[rg, :], big[pl.ds(GROUP * s, GROUP), 768:896], TN)
+        part += dot(attg[rg, :], heads[s, rg, 0:128], TN)
+        wt[3 * s, :, 768:896] = part.astype(bf16)
+        wt[3 * s, :, 896:D] = dot(attg[rg, :], heads[s, rg, 128:384], TN).astype(bf16)
 
     def heads_back(s, between):
-        mark("heads_grad")
         hgrad[:, 0:QUARTER] = dot(attg[...], wt[3 * s, 3 * QUARTER : D, :], NT).astype(bf16)
         facc[...] = jnp.zeros((2, ATT, 384), f32)
         dq_t[...] = jnp.zeros((384, ATT), f32)
         for i in range(5):
             keys_t[:, i * 128 : (i + 1) * 128] = qkv[s, 1, i * 128 : (i + 1) * 128, :].T
-        mark("attend_back")
         for_blocks(functools.partial(attend_back, s), between)
-        mark("pack")
         pack(s)
 
-    mark("rs_one_5")
-    rs_one(5)
-    mark("down_grad_0")
-    down_grad(0)
-    rs_core(2)
-    heads_back(1, (lambda: rs_two(4), lambda: rs_one(2)))
-    mark("first_far")
+    heads_back(1, (lambda: rs_three(4), lambda: rs_one(2)))
+    rs_two(5)
     lax.fori_loop(0, 6, first_far, 0)
-    mark("attn_grad_1")
+    rs_three(5)
     attn_grad(1)
     rs_core(3)
-    mark("rs_three_4")
-    rs_three(4)
-    rs_two(5)
-    mark("up_grad_0")
+    rs_two(2)
     up_grad(0)
     rs_core(1)
-    mark("rs_one_3")
     rs_one(3)
-    rs_two(2)
-    heads_back(0, (lambda: rs_three(5), lambda: rs_one(1)))
+    heads_back(0, (lambda: None, lambda: rs_one(1)))
+    rs_two(3)
     sent(("sec",))
-    mark("first_back")
     first_back(1 - low, 0)
     send(("first",), seco.at[pl.ds(0, OWN)], firstr, narrow_to(1))
-    mark("first_back_own")
     first_back(low, OWN)
-    mark("rs_two_3")
-    rs_two(3)
-    mark("attn_grad_0")
     attn_grad(0)
     rs_core(0)
-    mark("rs_three_21")
-    rs_three(2)
-    rs_two(1)
-    mark("rs_one_0")
-    rs_one(0)
-    mark("wait_mlp")
     recv(("mlp",), mlpr)
-    mark("mix")
     lax.fori_loop(0, OWN // 32, mix, 0)
     outs.append(load("mixed", mlpr, mixed_o))
-
-    mark("wait_first")
+    rs_three(2)
+    rs_one(0)
+    rs_three(3)
+    rs_two(1)
+
     recv(("first",), firstr)
-    allow(1)
-
-    mark("tokens_back")
+
     def tokens_back(t, carry):
         ra = rows_at(own_at + t * 32, 32, 32)
         rr = rows_at(t * 32, 32, 32)
@@ -783,13 +719,12 @@
         res = mgrad[rr, :] + norm_back(normal, scale, grad * (1.0 + mod_row(1, block)))
         firstr[rr, :] = res.astype(bf16)
         for k, v in ((0, grad), (1, grad * normal)):
-            msum[t // 4, k : k + 1, :] += jnp.sum(v, axis=0, keepdims=True)
+            msum[t // 4, k] += by_eight(v)
         return carry
 
     lax.fori_loop(0, OWN // 32, tokens_back, 0)
     outs.append(load("tg", firstr, tg_o))
 
-    mark("modgrad")
     sent(("mod",))
     row = lax.broadcasted_iota(jnp.int32, (8, D), 0)
     lane = lax.broadcasted_iota(jnp.int32, (8, ATT), 1)
@@ -797,7 +732,7 @@
         total = jnp.zeros((8, D), f32)
         for i in range(2):
             slot = seg[SEG * (4 * high + 2 * low + i)]
-            total += jnp.where((row == slot) & (row < 4), msum[i, k : k + 1, :], 0.0)
+            total += jnp.where((row == slot) & (row < 4), jnp.sum(msum[i, k], axis=0, keepdims=True), 0.0)
         for i, value in ((2 * k, total[:, 0:ATT]), (2 * k + 1, pltpu.roll(total[:, 512:D], HALF, 1))):
             modrecv[i // 3, i % 3 * 4 : i % 3 * 4 + 4, :] = jnp.where(lane < HALF, value, 0.0)[0:4, :]
     for i in range(4):
@@ -806,15 +741,10 @@
     for mask in (1, 2, 3):
         m = narrow_to(mask)[1]
         send(("mg", mask), mgs.at[m], mgr.at[mask - 1], narrow_to(mask))
-    mark("rs_three_3")
-    allowed(1)
-    rs_three(3)
     rs_three(1)
-    mark("rs_two_0")
     rs_two(0)
     rs_four(2)
     rs_four(1)
-    mark("wait_mg")
     for mask in (1, 2, 3):
         recv(("mg", mask), mgr.at[mask - 1])
     total = modrecv[n] + mgr[0].astype(f32) + mgr[1].astype(f32) + mgr[2].astype(f32)
@@ -822,22 +752,17 @@
     if gather_wide:
         for mask in range(1, 8):
             send(("mall", mask), mall.at[b], mall.at[b], wide_to(mask))
-    mark("rs_three_0")
     rs_three(0)
-    mark("rs_four_0")
     rs_four(0)
-    mark("wait_mall")
     if gather_wide:
         for mask in range(1, 8):
             recv(("silu", mask), silu_all.at[block_of(mask)])
             recv(("mall", mask), mall.at[block_of(mask)])
     outs.append(load("mall", mall, mall_o))
     outs.append(load("silu", silu_all, silu_o))
-    mark("drain")
     for copy in outs:
         copy.wait()
     sent(())
-    mark(None)
 
 
 def finish(
@@ -884,7 +809,7 @@
             if i == 0:
                 wada[:, HALF:640] = jnp.zeros((BLK, 64), f32)
     place = lax.axis_index("wide")
-    bada[...] = pltpu.roll(sums[...], 14 * 128 - place * QUARTER // 4 * 3, 1)[:, 0:256]
+    bada[...] = pltpu.roll(sums[...], 14 * 128 - place * 216, 1)[0:1, 0:216]
     outs.append(move(wada, wada_o))
     outs.append(move(bada, bada_o))
     ins[2].wait()
@@ -958,12 +883,11 @@
             V((6, 8, D), f32),
             V((4, 16, ATT), f32),
             V((8, 16, D), bf16),
-            V((2, 6, D), f32),
+            V((2, 6, 8, D), f32),
             V((4, 16, ATT), bf16),
             V((3, 16, ATT), bf16),
             V((8, 16, ATT), bf16),
             V((16, D), f32),
-            pltpu.SemaphoreType.REGULAR((2,)),
             pltpu.SemaphoreType.DMA((SEMS,)),
             pltpu.SemaphoreType.DMA((SEMS,)),
             pltpu.SemaphoreType.DMA((17,)),
@@ -991,7 +915,7 @@
             shape((OWN, D), bf16),
             shape((OWN, D), bf16),
             shape((BLK, 3 * HALF), f32),
-            shape((8, 256), f32),
+            shape((1, 216), f32),
             shape((3, BLK, QUARTER), f32),
             shape((BLK, QUARTER), f32),
             shape((BLK, D), f32),
@@ -1008,7 +932,7 @@
             V((OWN, D), bf16),
             V((BLK, 3 * HALF), f32),
             V((8, 14 * 128), f32),
-            V((8, 256), f32),
+            V((1, 216), f32),
             V((3, BLK, QUARTER), f32),
             V((BLK, QUARTER), f32),
             V((2, BLK, D), f32),
@@ -1019,7 +943,7 @@
     gqkv = gqkv.transpose(1, 0, 2)
     place = lax.axis_index("wide")
     if gather_wide:
-        w_ada_grad, b_ada_grad = wada, bada[0, : 3 * HALF // N]
+        w_ada_grad, b_ada_grad = wada, bada.reshape(216)
     else:
         silu_low = jax.nn.silu(condition.astype(f32)).astype(bf16)
         mine = lax.dynamic_index_in_dim(mall, place // step, keepdims=False)

time: 226 us -> 201 us (0.89)
  Pallas kernels: 223 us -> 198 us
    pallas_call x1, Pallas kernels: 218 us -> 194 us  [shards(): pl.pallas_call(functools.partial(kernel, gather_wide, step), name='block'...]
where the time goes in v3:
time: 201 us
  Pallas kernels  198 us (99%)
    pallas_call x1, Pallas kernels, shards(): pl.pallas_call(functools.partial(kernel, gather_wide, step), name='block'...  194 us
    pallas_call x1, Pallas kernels, shards(): pl.pallas_call(functools.partial(finish, step), name='finish', out_shape=...  4.7 us

profile of v3, /device:TPU:0, one launch (start us, length us, event | category | flops | bytes accessed | tf_op | source)
XLA Modules:
  0.0 200.7 jit_solution(8063331944584088655)
XLA Ops:
  0.6 1.4 reshape.32.bada
  2.0 193.8 %block.1 = (bf16[256,1152]{1,0:T(8,128)(2,1)}, bf16[256,1152]{1,0:T(8,128)(2,1)}, bf16[3,144,1152]{2,1,0:T(8,128)(2,1)}, bf16[3,144,1152]{2,1,0:T(8,128)(2,1)}, ...) custom-call(s32[1024]{0:T(1024)} %seg.1, bf16[4,1152]{1,0:T(4,128)(2,1)} %cond.1, f32[3,576]{1,0:T(4,128)} %reshape.32.bada, ...), custom_call_target="tpu_custom_call" | custom-call | tf_op jit(solution)/shard_map/block/pallas_call | solution.py:842
  195.8 4.7 %finish.1 = (bf16[256,1152]{1,0:T(8,128)(2,1)}, bf16[256,1152]{1,0:T(8,128)(2,1)}, f32[144,1728]{1,0:T(8,128)}, f32[1,216]{1,0:T(1,128)}, f32[3,144,288]{2,1,0:T...) custom-call(bf16[256,1152]{1,0:T(8,128)(2,1)} %get-tuple-element.22.mixed_h, ...), custom_call_target="tpu_custom_call" | custom-call | tf_op jit(solution)/shard_map/finish/pallas_call | solution.py:911

commit v4 on v3

--- a/solution.py
+++ b/solution.py
@@ -67,7 +67,7 @@
         return self.ids.setdefault(name, len(self.ids))
 
 
-SEMS = 122
+SEMS = 83
 
 
 def kernel(
@@ -116,10 +116,9 @@
 
     sends = {}
 
-    def send(name, src, dst, dev):
-        copy = remote(name, src, dst, dev)
-        copy.start()
-        sends[name] = copy
+    def send(name, src, dst, dev, group=None):
+        remote(name, src, dst, dev).start()
+        sends[name] = remote(name, src, dst, dev) if group is None else remote(name, group, group, dev)
 
     def recv(name, landing):
         remote(name, landing, landing, narrow_to(1)).wait_recv()
@@ -183,7 +182,8 @@
 
     def ag_pass(m, name, mask, axis, part=None):
         r = block_rows(mask, part)
-        send(("ag", m) + name, wt.at[3 + m, r], wt.at[3 + m, r], wide_to(axis))
+        group = wt.at[3 + m, pl.ds(0, 4 * BLK)] if axis == 1 else None
+        send(("ag", m) + name, wt.at[3 + m, r], wt.at[3 + m, r], wide_to(axis), group)
 
     def ag_take(m, name, mask, part=None):
         recv(("ag", m) + name, wt.at[3 + m, block_rows(mask, part)])
@@ -192,24 +192,23 @@
         ag_take(m, ("z",), 0)
         ag_pass(m, ("x",), 0, 2)
         ag_pass(m, ("y",), 0, 4)
-        ag_pass(m, ("c", 0), 0, 1)
+        ag_pass(m, ("c",), 0, 1)
 
     def ag_two(m):
         ag_take(m, ("x",), 2)
         ag_pass(m, ("xy",), 2, 4, 0)
         ag_take(m, ("y",), 4)
         ag_pass(m, ("yx",), 4, 2, 1)
-        ag_pass(m, ("c", 2), 2, 1)
-        ag_pass(m, ("c", 4), 4, 1)
+        ag_pass(m, ("c",), 2, 1)
+        ag_pass(m, ("c",), 4, 1)
 
     def ag_three(m):
         ag_take(m, ("xy",), 6, 0)
         ag_take(m, ("yx",), 6, 1)
-        ag_pass(m, ("c", 6), 6, 1)
+        ag_pass(m, ("c",), 6, 1)
 
     def ag_end(m):
-        for mask in (0, 2, 4, 6):
-            ag_take(m, ("c", mask), mask ^ 1)
+        recv(("ag", m, "c"), wt.at[3 + m, pl.ds(0, 4 * BLK)])
 
     for mask in (1, 2, 3):
         send(("mod", mask), modrecv.at[n], modrecv.at[n], narrow_to(mask))
@@ -341,11 +340,12 @@
 
         lax.fori_loop(2, 5, body, 0)
 
+    load_d.wait()
+    ag_two(0)
+    ag_z(2)
     project(0)
-    load_d.wait()
-    ag_z(2)
-    ag_two(0)
-    for_blocks(functools.partial(attend, 0), (lambda: None, lambda: ag_three(0)))
+    ag_three(0)
+    for_blocks(functools.partial(attend, 0))
     ag_one(1)
     ag_end(0)
     project(1)
@@ -356,7 +356,7 @@
 
     if gather_wide:
         for mask in range(1, 8):
-            send(("silu", mask), silu_all.at[b], silu_all.at[b], wide_to(mask))
+            send(("silu",), silu_all.at[b], silu_all.at[b], wide_to(mask), silu_all.at[pl.ds(0, 7)])
     for i in range(2):
         cc = order(i)
         src = rows_at(off + OWN * cc, OWN)
@@ -375,6 +375,7 @@
 
     ag_three(1)
     ag_one(2)
+    ag_two(2)
     recv(("og",), og.at[rows_at(OWN * (1 - low), OWN)])
 
     for i in range(2):
@@ -398,7 +399,6 @@
 
         lax.fori_loop(0, OWN // 32, second_norm, 0)
         if i == 0:
-            ag_two(2)
             ag_end(1)
 
         def units(k, carry):
@@ -415,11 +415,13 @@
             big[rows_at(2 * GROUP + GROUP * s + OWN * cc, OWN), cols] = (grad * slope).astype(bf16)
             return carry
 
-        lax.fori_loop(0, 3, units, 0)
         if i == 0:
+            lax.fori_loop(0, 3, units, 0)
             ag_three(2)
             ag_end(2)
-        lax.fori_loop(3, 6, units, 0)
+            lax.fori_loop(3, 6, units, 0)
+        else:
+            lax.fori_loop(0, 6, units, 0)
 
         def inputs_back(t, carry):
             cols = pl.ds(pl.multiple_of(t * 384, 128), 384)
@@ -433,33 +435,35 @@
 
     sent(("ag",))
 
-    def kept(mask):
-        return rows_at(block_of(mask) * BLK, BLK)
-
     def pieces(m):
         return ((pl.ds(0, 640), 2, 4), (pl.ds(640, 512), 4, 2))
 
+    def part(m, mask, cols=slice(None), start=0, size=BLK):
+        k = block_of(mask)
+        if m == 3:
+            return crecv.at[4 + k // 4, rows_at(k % 4 * BLK + start, size), cols]
+        return wt.at[m, rows_at(k * BLK + start, size), cols]
+
     def rs_core(m):
         for i, mask in enumerate((0, 2, 4, 6)):
-            send(("rs", m, "c", i), wt.at[m, kept(mask ^ 1)], crecv.at[m, pl.ds(i * BLK, BLK)], wide_to(1))
+            send(("rs", m, "c"), part(m, mask ^ 1), crecv.at[m, pl.ds(i * BLK, BLK)], wide_to(1), crecv.at[m])
 
     def add_into(m, mask, ref, at, cols):
         def body(t, carry):
-            r = rows_at(block_of(mask) * BLK + t * 48, 48)
-            wt[m, r, cols] = wt[m, r, cols] + ref[m, rows_at(at + t * 48, 48), cols]
+            mine = part(m, mask, cols, t * 48, 48)
+            mine[...] = mine[...] + ref[m, rows_at(at + t * 48, 48), cols]
             return carry
 
         lax.fori_loop(0, BLK // 48, body, 0)
 
     def rs_one(m):
-        for i, mask in enumerate((0, 2, 4, 6)):
-            recv(("rs", m, "c", i), crecv.at[m, pl.ds(i * BLK, BLK)])
+        recv(("rs", m, "c"), crecv.at[m])
         for p, (cols, first, second) in enumerate(pieces(m)):
             for mask in (first, 6):
                 add_into(m, mask, crecv, mask // 2 * BLK, cols)
             for i, mask in enumerate((0, second)):
                 send(
-                    ("rs", m, "f", p, i), wt.at[m, kept(mask ^ first), cols], frecv.at[m, pl.ds(i * BLK, BLK), cols],
+                    ("rs", m, "f", p, i), part(m, mask ^ first, cols), frecv.at[m, pl.ds(i * BLK, BLK), cols],
                     wide_to(first),
                 )
         for p, (cols, first, second) in enumerate(pieces(m)):
@@ -470,21 +474,31 @@
         for p, (cols, first, second) in enumerate(pieces(m)):
             recv(("rs", m, "f", p, 1), frecv.at[m, pl.ds(BLK, BLK), cols])
             add_into(m, second, frecv, BLK, cols)
-            send(("rs", m, "s", p), wt.at[m, kept(second), cols], srecv.at[m, :, cols], wide_to(second))
+            send(("rs", m, "s", p), part(m, second, cols), srecv.at[m, :, cols], wide_to(second))
         for p, (cols, first, second) in enumerate(pieces(m)):
             recv(("rs", m, "f", p, 0), frecv.at[m, pl.ds(0, BLK), cols])
             add_into(m, 0, frecv, 0, cols)
 
     outs = []
+
+    def rs_copy(m):
+        return remote(("rs", m, "z"), part(m, 0), zrecv.at[m - 3], narrow_to(2))
+
+    def rs_start(m, here):
+        @pl.when(here)
+        def _():
+            rs_copy(m).start()
 
     def rs_three(m):
         for p, (cols, _, _) in enumerate(pieces(m)):
             recv(("rs", m, "s", p), srecv.at[m, :, cols])
             add_into(m, 0, srecv, 0, cols)
         if m >= 3:
-            send(("rs", m, "z"), wt.at[m, kept(0)], zrecv.at[m - 3], narrow_to(2))
+            sends["rs", m, "z"] = rs_copy(m)
+            if m > 3:
+                rs_start(m, halo_source)
         else:
-            outs.append(load(("own", m), wt.at[m, kept(0)], gown_o.at[m]))
+            outs.append(load(("own", m), part(m, 0), gown_o.at[m]))
 
     def rs_four(m):
         recv(("rs", m + 3, "z"), zrecv.at[m])
@@ -497,26 +511,24 @@
         mlpp[:, :, cols] = part.astype(bf16).reshape(2, OWN, 384)
         return carry
 
-    def by_columns(fn, count, tail=None):
+    def by_columns(fn, count=5):
         def body(t, carry):
-            fn(pl.ds(pl.multiple_of(t * 256, 128), 256))
+            fn(pl.ds(pl.multiple_of(jnp.minimum(t * 256, D - 256), 128), 256))
             return carry
 
         lax.fori_loop(0, count, body, 0)
-        if tail is not None:
-            fn(pl.ds(tail, 128))
 
     def down_grad(s):
         def tile(cols):
             wt[3 * s + 2, :, cols] = dot(big[pl.ds(GROUP * s, GROUP), :], mlpg[:, cols], TN).astype(bf16)
 
-        by_columns(tile, 4, 1024)
+        by_columns(tile)
 
     def up_grad(s):
         def tile(cols):
             wt[3 * s + 1, :, cols] = dot(h2[...], big[pl.ds(2 * GROUP + GROUP * s, GROUP), cols], TN).astype(bf16)
 
-        by_columns(tile, 4, 1024)
+        by_columns(tile)
 
     up_grad(1)
     rs_core(4)
@@ -572,9 +584,7 @@
             r = rows_at(halo_at + 64 * low, 64)
             recv(("ahalo", 0), attg.at[r])
             send(("ahalo", 1), attg.at[r], attg.at[r], narrow_to(1))
-
-    recv(("ahalo", 1), attg.at[rows_at(halo_at + 64 * (1 - low), 64)])
-    send(("mlp",), mlpp.at[1 - low], mlpr, narrow_to(1))
+            send(("mlp",), mlpp.at[1 - low], mlpr, narrow_to(1))
 
     def mix(t, carry):
         r = rows_at(OWN * low + t * 32, 32, 32)
@@ -642,73 +652,93 @@
 
         lax.fori_loop(0, GROUP // 128, body, 0)
 
-    def first_far(t, carry):
-        half, cols = t // 3, pl.ds(pl.multiple_of(t % 3 * 384, 128), 384)
-        part = dot(big[rows_at(GROUP + OWN * half, OWN), 0 : 3 * QUARTER], wt[3, 0 : 3 * QUARTER, cols], NN)
-        high_part = part.astype(bf16)
-        secr[rows_at(OWN * half, OWN), cols] = high_part
-        mlpg[rows_at(OWN * half, OWN), cols] = (part - high_part.astype(f32)).astype(bf16)
-        return carry
-
     def first_back(half, at):
-        def body(t, carry):
-            cols = pl.ds(pl.multiple_of(t * 384, 128), 384)
-            part = dot(big[rows_at(OWN * half, OWN), 0 : 3 * QUARTER], wt[0, 0 : 3 * QUARTER, cols], NN)
-            part += secr[rows_at(OWN * half, OWN), cols].astype(f32)
-            part += mlpg[rows_at(OWN * half, OWN), cols].astype(f32)
-            seco[pl.ds(at, OWN), cols] = part.astype(bf16)
-            return carry
-
-        lax.fori_loop(0, 3, body, 0)
+        def tile(cols):
+            total = dot(big[rows_at(OWN * half, OWN), 0 : 3 * QUARTER], wt[0, 0 : 3 * QUARTER, cols], NN)
+            total += dot(big[rows_at(GROUP + OWN * half, OWN), 0 : 3 * QUARTER], wt[3, 0 : 3 * QUARTER, cols], NN)
+            seco[pl.ds(at, OWN), cols] = total.astype(bf16)
+
+        by_columns(tile)
 
     def attn_grad(s):
         rg = rows_at(off, GROUP)
 
+        def put(cols, value):
+            value = value.astype(bf16)
+            if s == 0:
+                wt[0, :, cols] = value
+            else:
+                crecv[4, :, cols] = value[: 4 * BLK, :]
+                crecv[5, :, cols] = value[4 * BLK :, :]
+
         def tile(cols):
-            wt[3 * s, :, cols] = dot(h1[rg, :], big[pl.ds(GROUP * s, GROUP), cols], TN).astype(bf16)
+            put(cols, dot(h1[rg, :], big[pl.ds(GROUP * s, GROUP), cols], TN))
 
         by_columns(tile, 3)
-        part = dot(h1[rg, :], big[pl.ds(GROUP * s, GROUP), 768:896], TN)
-        part += dot(attg[rg, :], heads[s, rg, 0:128], TN)
-        wt[3 * s, :, 768:896] = part.astype(bf16)
-        wt[3 * s, :, 896:D] = dot(attg[rg, :], heads[s, rg, 128:384], TN).astype(bf16)
-
-    def heads_back(s, between):
-        hgrad[:, 0:QUARTER] = dot(attg[...], wt[3 * s, 3 * QUARTER : D, :], NT).astype(bf16)
+        value = dot(h1[rg, :], big[pl.ds(GROUP * s, GROUP), 768:896], TN)
+        value += dot(attg[rg, :], heads[s, rg, 0:128], TN)
+        put(slice(768, 896), value)
+        put(slice(896, D), dot(attg[rg, :], heads[s, rg, 128:384], TN))
+
+    def heads_rows(s, r):
+        hgrad[r, 0:QUARTER] = dot(attg[r, :], wt[3 * s, 3 * QUARTER : D, :], NT).astype(bf16)
+
+    def heads_back(s, early, middle):
+        heads_rows(s, rows_at(off, GROUP))
         facc[...] = jnp.zeros((2, ATT, 384), f32)
         dq_t[...] = jnp.zeros((384, ATT), f32)
         for i in range(5):
             keys_t[:, i * 128 : (i + 1) * 128] = qkv[s, 1, i * 128 : (i + 1) * 128, :].T
-        for_blocks(functools.partial(attend_back, s), between)
+        attend_back(s, 1, 0, 5)
+        early()
+
+        def body(j, carry):
+            attend_back(s, j, 1, 4)
+            return carry
+
+        lax.fori_loop(2, 4, body, 0)
+        middle()
+        heads_rows(s, rows_at(halo_at, SEG))
+        attend_back(s, 0, 0, 2)
+        attend_back(s, 4, 1, 4)
         pack(s)
 
-    heads_back(1, (lambda: rs_three(4), lambda: rs_one(2)))
-    rs_two(5)
-    lax.fori_loop(0, 6, first_far, 0)
-    rs_three(5)
+    def middle_far():
+        recv(("ahalo", 1), attg.at[rows_at(halo_at + 64 * (1 - low), 64)])
+        rs_start(4, jnp.logical_not(halo_source))
+        rs_two(5)
+
+
+    rs_three(4)
+    heads_back(1, lambda: None, middle_far)
+    rs_one(2)
     attn_grad(1)
     rs_core(3)
-    rs_two(2)
+    rs_three(5)
     up_grad(0)
     rs_core(1)
     rs_one(3)
-    heads_back(0, (lambda: None, lambda: rs_one(1)))
-    rs_two(3)
+    rs_start(5, jnp.logical_not(halo_source))
+    heads_back(0, lambda: None, lambda: None)
+    rs_two(2)
+    rs_one(1)
     sent(("sec",))
     first_back(1 - low, 0)
     send(("first",), seco.at[pl.ds(0, OWN)], firstr, narrow_to(1))
     first_back(low, OWN)
+    rs_two(3)
     attn_grad(0)
     rs_core(0)
+    rs_three(2)
     recv(("mlp",), mlpr)
     lax.fori_loop(0, OWN // 32, mix, 0)
     outs.append(load("mixed", mlpr, mixed_o))
-    rs_three(2)
     rs_one(0)
     rs_three(3)
     rs_two(1)
 
     recv(("first",), firstr)
+    rs_start(3, jnp.logical_not(halo_source))
 
     def tokens_back(t, carry):
         ra = rows_at(own_at + t * 32, 32, 32)
@@ -747,17 +777,17 @@
     rs_four(1)
     for mask in (1, 2, 3):
         recv(("mg", mask), mgr.at[mask - 1])
+    rs_start(3, halo_source)
     total = modrecv[n] + mgr[0].astype(f32) + mgr[1].astype(f32) + mgr[2].astype(f32)
     mall[b] = total.astype(bf16)
     if gather_wide:
         for mask in range(1, 8):
-            send(("mall", mask), mall.at[b], mall.at[b], wide_to(mask))
+            send(("mall",), mall.at[b], mall.at[b], wide_to(mask), mall.at[pl.ds(0, 7)])
     rs_three(0)
     rs_four(0)
     if gather_wide:
-        for mask in range(1, 8):
-            recv(("silu", mask), silu_all.at[block_of(mask)])
-            recv(("mall", mask), mall.at[block_of(mask)])
+        recv(("silu",), silu_all.at[pl.ds(0, 7)])
+        recv(("mall",), mall.at[pl.ds(0, 7)])
     outs.append(load("mall", mall, mall_o))
     outs.append(load("silu", silu_all, silu_o))
     for copy in outs:
@@ -780,10 +810,6 @@
     ins = [move(mall_h, mall), move(silu_h, silu), move(gown_h, gown), move(gfar_h, gfar)]
     outs = []
     rows = [move(mixed_h, mixed), move(tg_h, tg)]
-    rows[0].wait()
-    outs.append(move(mixed, mixed_o))
-    rows[1].wait()
-    outs.append(move(tg, tg_o))
     b = lax.axis_index("wide") // step
     ins[0].wait()
     ins[1].wait()
@@ -826,6 +852,10 @@
         else:
             gffn[m - 1] = total
             outs.append(move(gffn.at[m - 1], (gup_o, gdown_o)[m - 1]))
+    rows[0].wait()
+    outs.append(move(mixed, mixed_o))
+    rows[1].wait()
+    outs.append(move(tg, tg_o))
     for copy in outs:
         copy.wait()
 

time: 201 us -> 198 us (0.985)
  Pallas kernels: 198 us -> 195 us
    pallas_call x1, Pallas kernels: 194 us -> 191 us  [shards(): pl.pallas_call(functools.partial(kernel, gather_wide, step), name='block'...]
where the time goes in v4:
time: 198 us
  Pallas kernels  195 us (98%)
    pallas_call x1, Pallas kernels, shards(): pl.pallas_call(functools.partial(kernel, gather_wide, step), name='block'...  191 us
    pallas_call x1, Pallas kernels, shards(): pl.pallas_call(functools.partial(finish, step), name='finish', out_shape=...  4.11 us

profile of v4, /device:TPU:0, one launch (start us, length us, event | category | flops | bytes accessed | tf_op | source)
XLA Modules:
  0.0 197.7 jit_solution(6545554256904835046)
XLA Ops:
  0.6 1.4 reshape.32.bada
  2.0 191.4 %block.1 = (bf16[256,1152]{1,0:T(8,128)(2,1)}, bf16[256,1152]{1,0:T(8,128)(2,1)}, bf16[3,144,1152]{2,1,0:T(8,128)(2,1)}, bf16[3,144,1152]{2,1,0:T(8,128)(2,1)}, ...) custom-call(s32[1024]{0:T(1024)} %seg.1, bf16[4,1152]{1,0:T(4,128)(2,1)} %cond.1, f32[3,576]{1,0:T(4,128)} %reshape.32.bada, ...), custom_call_target="tpu_custom_call" | custom-call | tf_op jit(solution)/shard_map/block/pallas_call | solution.py:872
  193.4 4.1 %finish.1 = (bf16[256,1152]{1,0:T(8,128)(2,1)}, bf16[256,1152]{1,0:T(8,128)(2,1)}, f32[144,1728]{1,0:T(8,128)}, f32[1,216]{1,0:T(1,128)}, f32[3,144,288]{2,1,0:T...) custom-call(bf16[256,1152]{1,0:T(8,128)(2,1)} %get-tuple-element.22.mixed_h, ...), custom_call_target="tpu_custom_call" | custom-call | tf_op jit(solution)/shard_map/finish/pallas_call | solution.py:941

commit v5 on v4

--- a/solution.py
+++ b/solution.py
@@ -75,7 +75,7 @@
     seg, cond, bada, tok_h, og_h, wada_h, wqkv_h, wproj_h, wup_h, wdown_h,
     mixed_o, tg_o, gown_o, gfar_o, mall_o, silu_o,
     wt, crecv, frecv, srecv, zrecv, tok, og, h1, qkv, heads, lse_t, attp, attr, h2, mlpg, big,
-    mlpp, mlpr, seco, secr, mgrad, attg, hgrad, facc, keys_t, dq_t, firstr, modblk, modrecv, silu_all, msum, mgs, mgr, mall, silu16,
+    mlpp, mlpr, seco, secr, mgrad, attg, hgrad, facc, keys_t, dq_t, firstr, modblk, modrecv, silu_all, msum, msum_one, mgs, mgr, mall, silu16,
     ssem, rsem, lsem,
 ):
     w = lax.axis_index("wide")
@@ -163,7 +163,7 @@
     third = lax.broadcasted_iota(jnp.int32, (16, HALF), 0) // 4
     part = jnp.zeros((16, HALF), f32)
     for i in range(3):
-        value = dot(silu_low, big[HALF * i : HALF * (i + 1), :], NT) + bada[i : i + 1, :]
+        value = dot(silu_low, big[HALF * i : HALF * (i + 1), :], NT) + bada[pl.ds(HALF * i, HALF)].astype(f32).reshape(1, HALF)
         part = jnp.where(third == i, value, part)
     modrecv[n, :, 0:HALF] = part
     modrecv[n, :, HALF:ATT] = jnp.zeros((16, ATT - HALF), f32)
@@ -251,6 +251,15 @@
 
         lax.fori_loop(0, size // 32, body, 0)
 
+    def project(s, base=0, size=ATT):
+        r = rows_at(base, size, SEG)
+
+        def body(i, carry):
+            qkv[s, i, r, :] = dot(h1[r, :], wt[3 * s, rows_at(QUARTER * i, 384), :], NT).astype(bf16)
+            return carry
+
+        lax.fori_loop(0, 3, body, 0)
+
     load_t.wait()
     first_norm(own_at, OWN)
 
@@ -259,6 +268,7 @@
         halo_first.wait_recv()
         halo_second.start()
 
+    project(0, own_at, OWN)
     ag_one(0)
     load_u.wait()
     ag_z(1)
@@ -272,18 +282,12 @@
         halo_second.wait_recv()
         halo_first.wait_send()
 
+    project(0, other_at, OWN)
     first_norm(halo_at, SEG)
 
     @pl.when(jnp.logical_not(halo_source))
     def _():
         halo_second.wait_send()
-
-    def project(s):
-        def body(i, carry):
-            qkv[s, i] = dot(h1[...], wt[3 * s, rows_at(QUARTER * i, 384), :], NT).astype(bf16)
-            return carry
-
-        lax.fori_loop(0, 3, body, 0)
 
     def key_bias(j, k0, count):
         mine = seg[SEG * (j + 3 * high)]
@@ -343,9 +347,8 @@
     load_d.wait()
     ag_two(0)
     ag_z(2)
-    project(0)
-    ag_three(0)
-    for_blocks(functools.partial(attend, 0))
+    project(0, halo_at, SEG)
+    for_blocks(functools.partial(attend, 0), (lambda: None, lambda: ag_three(0)))
     ag_one(1)
     ag_end(0)
     project(1)
@@ -532,7 +535,8 @@
 
     up_grad(1)
     rs_core(4)
-    msum[...] = jnp.zeros((2, 6, 8, D), f32)
+    msum[...] = jnp.zeros((2, 4, 8, D), f32)
+    msum_one[...] = jnp.zeros((4, 2, 8, D), f32)
     for i in range(2):
         cc = order(i)
         chunk = rows_at(OWN * cc, OWN)
@@ -557,7 +561,7 @@
                 mgrad[rows_at(t * 32, 32, 32), :] = mid
                 at = t // 4
                 for k, v in ((2, mid * branch), (3, grad), (4, grad * normal)):
-                    msum[at, k] += by_eight(v)
+                    msum[at, k - 2] += by_eight(v)
                 return carry
 
             lax.fori_loop(0, OWN // 32, body, 0)
@@ -595,7 +599,7 @@
         middle = tok[ra, :].astype(f32) + mod_row(2, block) * branch
         mlp = mlpp[low, rr, :].astype(f32) + mlpr[rr, :].astype(f32)
         mlpr[rr, :] = (middle + mod_row(5, block) * mlp).astype(bf16)
-        msum[t // 4, 5] += by_eight(og[r, :].astype(f32) * mlp)
+        msum[t // 4, 3] += by_eight(og[r, :].astype(f32) * mlp)
         return carry
 
     def attend_back(s, j, k0, count):
@@ -719,9 +723,7 @@
     rs_core(1)
     rs_one(3)
     rs_start(5, jnp.logical_not(halo_source))
-    heads_back(0, lambda: None, lambda: None)
-    rs_two(2)
-    rs_one(1)
+    heads_back(0, lambda: None, lambda: (rs_two(2), rs_one(1)))
     sent(("sec",))
     first_back(1 - low, 0)
     send(("first",), seco.at[pl.ds(0, OWN)], firstr, narrow_to(1))
@@ -733,12 +735,40 @@
     recv(("mlp",), mlpr)
     lax.fori_loop(0, OWN // 32, mix, 0)
     outs.append(load("mixed", mlpr, mixed_o))
+
+    def first_sums(t, carry):
+        half = 1 - low + t // 8 * (2 * low - 1)
+        normal, _ = norm_parts(tok[rows_at(off + OWN * half + t % 8 * 32, 32, 32), :].astype(f32))
+        grad = seco[rows_at(t * 32, 32, 32), :].astype(f32)
+        msum_one[t // 4, 0] += by_eight(grad)
+        msum_one[t // 4, 1] += by_eight(grad * normal)
+        return carry
+
+    lax.fori_loop(0, GROUP // 32, first_sums, 0)
+    sent(("mod",))
+    row = lax.broadcasted_iota(jnp.int32, (8, D), 0)
+    lane = lax.broadcasted_iota(jnp.int32, (8, ATT), 1)
+    for k in range(6):
+        total = jnp.zeros((8, D), f32)
+        for i in range(4 if k < 2 else 2):
+            half, value = (low, msum[i, k - 2]) if k > 1 else (low if i > 1 else 1 - low, msum_one[i, k])
+            slot = seg[SEG * (4 * high + 2 * half + i % 2)]
+            total += jnp.where((row == slot) & (row < 4), jnp.sum(value, axis=0, keepdims=True), 0.0)
+        for i, value in ((2 * k, total[:, 0:ATT]), (2 * k + 1, pltpu.roll(total[:, 512:D], HALF, 1))):
+            modrecv[i // 3, i % 3 * 4 : i % 3 * 4 + 4, :] = jnp.where(lane < HALF, value, 0.0)[0:4, :]
+    for i in range(4):
+        modrecv[i, 12:16, :] = jnp.zeros((4, ATT), f32)
+        mgs[i] = modrecv[i].astype(bf16)
+    for mask in (1, 2, 3):
+        m = narrow_to(mask)[1]
+        send(("mg", mask), mgs.at[m], mgr.at[mask - 1], narrow_to(mask))
     rs_one(0)
     rs_three(3)
+    rs_start(3, jnp.logical_not(halo_source))
     rs_two(1)
 
     recv(("first",), firstr)
-    rs_start(3, jnp.logical_not(halo_source))
+    rs_start(3, halo_source)
 
     def tokens_back(t, carry):
         ra = rows_at(own_at + t * 32, 32, 32)
@@ -748,41 +778,22 @@
         grad = seco[rows_at(OWN + t * 32, 32, 32), :].astype(f32) + firstr[rr, :].astype(f32)
         res = mgrad[rr, :] + norm_back(normal, scale, grad * (1.0 + mod_row(1, block)))
         firstr[rr, :] = res.astype(bf16)
-        for k, v in ((0, grad), (1, grad * normal)):
-            msum[t // 4, k] += by_eight(v)
         return carry
 
     lax.fori_loop(0, OWN // 32, tokens_back, 0)
     outs.append(load("tg", firstr, tg_o))
-
-    sent(("mod",))
-    row = lax.broadcasted_iota(jnp.int32, (8, D), 0)
-    lane = lax.broadcasted_iota(jnp.int32, (8, ATT), 1)
-    for k in range(6):
-        total = jnp.zeros((8, D), f32)
-        for i in range(2):
-            slot = seg[SEG * (4 * high + 2 * low + i)]
-            total += jnp.where((row == slot) & (row < 4), jnp.sum(msum[i, k], axis=0, keepdims=True), 0.0)
-        for i, value in ((2 * k, total[:, 0:ATT]), (2 * k + 1, pltpu.roll(total[:, 512:D], HALF, 1))):
-            modrecv[i // 3, i % 3 * 4 : i % 3 * 4 + 4, :] = jnp.where(lane < HALF, value, 0.0)[0:4, :]
-    for i in range(4):
-        modrecv[i, 12:16, :] = jnp.zeros((4, ATT), f32)
-        mgs[i] = modrecv[i].astype(bf16)
-    for mask in (1, 2, 3):
-        m = narrow_to(mask)[1]
-        send(("mg", mask), mgs.at[m], mgr.at[mask - 1], narrow_to(mask))
-    rs_three(1)
-    rs_two(0)
-    rs_four(2)
-    rs_four(1)
     for mask in (1, 2, 3):
         recv(("mg", mask), mgr.at[mask - 1])
-    rs_start(3, halo_source)
     total = modrecv[n] + mgr[0].astype(f32) + mgr[1].astype(f32) + mgr[2].astype(f32)
     mall[b] = total.astype(bf16)
     if gather_wide:
         for mask in range(1, 8):
             send(("mall",), mall.at[b], mall.at[b], wide_to(mask), mall.at[pl.ds(0, 7)])
+
+    rs_two(0)
+    rs_three(1)
+    rs_four(2)
+    rs_four(1)
     rs_three(0)
     rs_four(0)
     if gather_wide:
@@ -913,7 +924,8 @@
             V((6, 8, D), f32),
             V((4, 16, ATT), f32),
             V((8, 16, D), bf16),
-            V((2, 6, 8, D), f32),
+            V((2, 4, 8, D), f32),
+            V((4, 2, 8, D), f32),
             V((4, 16, ATT), bf16),
             V((3, 16, ATT), bf16),
             V((8, 16, ATT), bf16),
@@ -928,7 +940,7 @@
     )(
         segment,
         condition,
-        b_ada.astype(f32).reshape(3, HALF),
+        b_ada,
         tokens,
         out_grad,
         w_ada.T,

time: 198 us -> 193 us (0.975)
  Pallas kernels: 195 us -> 192 us
    pallas_call x1, Pallas kernels: 191 us -> 188 us  [shards(): pl.pallas_call(functools.partial(kernel, gather_wide, step), name='block'...]
where the time goes in v5:
time: 193 us
  Pallas kernels  192 us (99%)
    pallas_call x1, Pallas kernels, shards(): pl.pallas_call(functools.partial(kernel, gather_wide, step), name='block'...  188 us
    pallas_call x1, Pallas kernels, shards(): pl.pallas_call(functools.partial(finish, step), name='finish', out_shape=...  4.11 us

profile of v5, /device:TPU:0, one launch (start us, length us, event | category | flops | bytes accessed | tf_op | source)
XLA Modules:
  0.0 192.8 jit_solution(12065972002780791502)
XLA Ops:
  0.6 187.9 %block.1 = (bf16[256,1152]{1,0:T(8,128)(2,1)}, bf16[256,1152]{1,0:T(8,128)(2,1)}, bf16[3,144,1152]{2,1,0:T(8,128)(2,1)}, bf16[3,144,1152]{2,1,0:T(8,128)(2,1)}, ...) custom-call(s32[1024]{0:T(1024)} %seg.1, bf16[4,1152]{1,0:T(4,128)(2,1)} %cond.1, bf16[1728]{0:T(1024)(128)(2,1)} %bada.1, ...), custom_call_target="tpu_custom_call" | custom-call | tf_op jit(solution)/shard_map/block/pallas_call | solution.py:883
  188.5 4.1 %finish.1 = (bf16[256,1152]{1,0:T(8,128)(2,1)}, bf16[256,1152]{1,0:T(8,128)(2,1)}, f32[144,1728]{1,0:T(8,128)}, f32[1,216]{1,0:T(1,128)}, f32[3,144,288]{2,1,0:T...) custom-call(bf16[256,1152]{1,0:T(8,128)(2,1)} %get-tuple-element.22.mixed_h, ...), custom_call_target="tpu_custom_call" | custom-call | tf_op jit(solution)/shard_map/finish/pallas_call | solution.py:953

commit v6 on v5

--- a/solution.py
+++ b/solution.py
@@ -766,9 +766,17 @@
     rs_three(3)
     rs_start(3, jnp.logical_not(halo_source))
     rs_two(1)
+    rs_start(3, halo_source)
+    rs_two(0)
+    for mask in (1, 2, 3):
+        recv(("mg", mask), mgr.at[mask - 1])
+    total = modrecv[n] + mgr[0].astype(f32) + mgr[1].astype(f32) + mgr[2].astype(f32)
+    mall[b] = total.astype(bf16)
+    if gather_wide:
+        for mask in range(1, 8):
+            send(("mall",), mall.at[b], mall.at[b], wide_to(mask), mall.at[pl.ds(0, 7)])
 
     recv(("first",), firstr)
-    rs_start(3, halo_source)
 
     def tokens_back(t, carry):
         ra = rows_at(own_at + t * 32, 32, 32)
@@ -782,15 +790,6 @@
 
     lax.fori_loop(0, OWN // 32, tokens_back, 0)
     outs.append(load("tg", firstr, tg_o))
-    for mask in (1, 2, 3):
-        recv(("mg", mask), mgr.at[mask - 1])
-    total = modrecv[n] + mgr[0].astype(f32) + mgr[1].astype(f32) + mgr[2].astype(f32)
-    mall[b] = total.astype(bf16)
-    if gather_wide:
-        for mask in range(1, 8):
-            send(("mall",), mall.at[b], mall.at[b], wide_to(mask), mall.at[pl.ds(0, 7)])
-
-    rs_two(0)
     rs_three(1)
     rs_four(2)
     rs_four(1)
@@ -818,12 +817,30 @@
         copy.start()
         return copy
 
-    ins = [move(mall_h, mall), move(silu_h, silu), move(gown_h, gown), move(gfar_h, gfar)]
+    ins = [move(gown_h, gown), move(gfar_h, gfar), move(mall_h, mall), move(silu_h, silu)]
     outs = []
     rows = [move(mixed_h, mixed), move(tg_h, tg)]
     b = lax.axis_index("wide") // step
     ins[0].wait()
     ins[1].wait()
+    for m in range(3):
+        total = gown[m].astype(f32) + gfar[m].astype(f32)
+        if m == 0:
+            gqkv[0] = total[:, 0:QUARTER]
+            gqkv[1] = pltpu.roll(total[:, 256:640], 352, 1)[:, 0:QUARTER]
+            gqkv[2] = pltpu.roll(total[:, 512:896], 320, 1)[:, 0:QUARTER]
+            gproj[...] = pltpu.roll(total[:, 768:D], 288, 1)[:, 0:QUARTER]
+            outs.append(move(gqkv, gqkv_o))
+            outs.append(move(gproj, gproj_o))
+        else:
+            gffn[m - 1] = total
+            outs.append(move(gffn.at[m - 1], (gup_o, gdown_o)[m - 1]))
+    rows[0].wait()
+    outs.append(move(mixed, mixed_o))
+    rows[1].wait()
+    outs.append(move(tg, tg_o))
+    ins[2].wait()
+    ins[3].wait()
     pick_row = lax.broadcasted_iota(jnp.int32, (BLK, D), 0) + b * BLK
     pick_col = lax.broadcasted_iota(jnp.int32, (BLK, D), 1)
     pick = jnp.where(pick_row == pick_col, 1.0, 0.0).astype(bf16)
@@ -849,24 +866,6 @@
     bada[...] = pltpu.roll(sums[...], 14 * 128 - place * 216, 1)[0:1, 0:216]
     outs.append(move(wada, wada_o))
     outs.append(move(bada, bada_o))
-    ins[2].wait()
-    ins[3].wait()
-    for m in range(3):
-        total = gown[m].astype(f32) + gfar[m].astype(f32)
-        if m == 0:
-            gqkv[0] = total[:, 0:QUARTER]
-            gqkv[1] = pltpu.roll(total[:, 256:640], 352, 1)[:, 0:QUARTER]
-            gqkv[2] = pltpu.roll(total[:, 512:896], 320, 1)[:, 0:QUARTER]
-            gproj[...] = pltpu.roll(total[:, 768:D], 288, 1)[:, 0:QUARTER]
-            outs.append(move(gqkv, gqkv_o))
-            outs.append(move(gproj, gproj_o))
-        else:
-            gffn[m - 1] = total
-            outs.append(move(gffn.at[m - 1], (gup_o, gdown_o)[m - 1]))
-    rows[0].wait()
-    outs.append(move(mixed, mixed_o))
-    rows[1].wait()
-    outs.append(move(tg, tg_o))
     for copy in outs:
         copy.wait()
 

time: 193 us -> 189 us (0.979)
  Pallas kernels: 192 us -> 187 us
    pallas_call x1, Pallas kernels: 188 us -> 184 us  [shards(): pl.pallas_call(functools.partial(kernel, gather_wide, step), name='block'...]
where the time goes in v6:
time: 189 us; the launch traced here: 188 us
  Pallas kernels  187 us (99%)
    pallas_call x1, Pallas kernels, shards(): pl.pallas_call(functools.partial(kernel, gather_wide, step), name='block'...  184 us
    pallas_call x1, Pallas kernels, shards(): pl.pallas_call(functools.partial(finish, step), name='finish', out_shape=...  3.93 us

profile of v6, /device:TPU:0, one launch (start us, length us, event | category | flops | bytes accessed | tf_op | source)
XLA Modules:
  0.0 188.3 jit_solution(8261142910384167063)
XLA Ops:
  0.6 183.6 %block.1 = (bf16[256,1152]{1,0:T(8,128)(2,1)}, bf16[256,1152]{1,0:T(8,128)(2,1)}, bf16[3,144,1152]{2,1,0:T(8,128)(2,1)}, bf16[3,144,1152]{2,1,0:T(8,128)(2,1)}, ...) custom-call(s32[1024]{0:T(1024)} %seg.1, bf16[4,1152]{1,0:T(4,128)(2,1)} %cond.1, bf16[1728]{0:T(1024)(128)(2,1)} %bada.1, ...), custom_call_target="tpu_custom_call" | custom-call | tf_op jit(solution)/shard_map/block/pallas_call | solution.py:882
  184.2 3.9 %finish.1 = (bf16[256,1152]{1,0:T(8,128)(2,1)}, bf16[256,1152]{1,0:T(8,128)(2,1)}, f32[144,1728]{1,0:T(8,128)}, f32[1,216]{1,0:T(1,128)}, f32[3,144,288]{2,1,0:T...) custom-call(bf16[256,1152]{1,0:T(8,128)(2,1)} %get-tuple-element.22.mixed_h, ...), custom_call_target="tpu_custom_call" | custom-call | tf_op jit(solution)/shard_map/finish/pallas_call | solution.py:952
